TPU v7x, 128 devices: a whole 4x4x4 slice. The times are simulated.
128 devices in a mesh: row: 8 (over z, core), col: 16 (over y, x).
Axes of the slice: x: 4, y: 4, z: 4, core: 2. Of those that a mesh axis runs over, the one named last changes fastest.
Arguments:
- densities: bfloat16 [128, 3, 256, 128], P(('row', 'col')), may hold values from -6 to 6
- positions: float32 [128, 3, 256], replicated, may hold values from -1 to 1
- areas: float32 [128, 256], replicated, may hold values from 0.15 to 0.6
- bases: bfloat16 [128, 32, 3, 256], P(('row', 'col')), may hold values from -0.21875 to 0.21875
- near_pairs: int32 [1920, 2], replicated, may hold values from 0 to 127, as said below
- far_pairs: int32 [768, 2], replicated, may hold values from 0 to 127
- couplings: bfloat16 [768, 1024], replicated, may hold values from -1 to 1
Outputs:
- potentials: bfloat16 [128, 3, 256, 128], P(('row', 'col'))
Inputs may be any that keep to these rules, and one draw needn't show every extreme that they name: `near_pairs`: cluster g is held by the device of mesh row (g) // 16 and mesh column (g) % 16. For each mesh row i and column j, at most 40 rows (t, s) have t held in mesh row i and s held in mesh column j, and some (i, j) has exactly 40.
All inputs are finite; a program needn't handle non-finite values.
Results may differ from a plain program's by a relative error of at most 0.005.
Values may be sent and summed in bfloat16 or wider, within the bound.
No kernel may reach another device: no remote copies, remote signals or barrier semaphores. Data moves between devices by JAX's collectives and lax.ppermute only.
A program may use at most 128 MiB of HBM per device.

v0:
```python
import functools

import jax
import jax.numpy as jnp
from jax import lax
from jax.experimental import pallas as pl
from jax.experimental.pallas import tpu as pltpu
from jax.sharding import PartitionSpec as P


CS = 256
LOADS = 128
RANK = 32
HALF = CS // 2
DENS = 3 * HALF
UNIT = 2 * DENS + RANK
FULL = 3 * CS + RANK
AXES = ("row", "col")
TARGETS = ((1, 0), (2, 0), (3, 0), (1, 1), (2, 1), (3, 1), (0, 0), (0, 1))
AWAY = 6
SPANS = {"first": (0, AWAY), "middle": (0, AWAY), "send": (3, AWAY), "keep": (0, 3), "own": (AWAY, 8)}
SIDE = 4

eps_square = 0.0004
lame_ratio = 1.8
kelvin_coef = 1.0 / (16.0 * 3.141592653589793 * 0.7)
VMEM_LIMIT = 16 * 1024 * 1024
bf16 = jnp.bfloat16
f32 = jnp.float32


def routes(move):
    pairs = []
    for z in range(SIDE):
        for core in range(2):
            for y in range(SIDE):
                for x in range(SIDE):
                    to_z, to_core, to_y, to_x = move(z, core, y, x)
                    source = (z * 2 + core) * 16 + y * SIDE + x
                    target = ((to_z % SIDE) * 2 + to_core) * 16 + (to_y % SIDE) * SIDE + to_x % SIDE
                    pairs.append((source, target))
    return pairs


def swap_core(value):
    return lax.ppermute(value, AXES, routes(lambda z, c, y, x: (z, 1 - c, y, x)))


def along_first(value, step):
    move = lambda z, c, y, x: (z, c, y, x + step) if c == 0 else (z, c, y + step, x)
    return lax.ppermute(value, AXES, routes(move))


def along_second(value, step):
    move = lambda z, c, y, x: (z, c, y + step, x) if c == 0 else (z, c, y, x + step)
    return lax.ppermute(value, AXES, routes(move))


def along_z(value, step):
    return lax.ppermute(value, AXES, routes(lambda z, c, y, x: (z + step, c, y, x)))


def whole(count):
    return [pl.BlockSpec(memory_space=pltpu.VMEM)] * count


def dot32(a, b):
    return jnp.dot(a, b, preferred_element_type=f32)


def iota(shape, dim):
    return lax.broadcasted_iota(jnp.int32, shape, dim)


def fetch(source, target, sem):
    copy = pltpu.make_async_copy(source, target, sem)
    copy.start()
    return copy


def moments_kernel(core_ref, dens_ref, bases_ref, own_ref, moments_ref, flip_ref, dens, bases, sems):
    copies = [fetch(dens_ref, dens, sems.at[0]), fetch(bases_ref, bases, sems.at[1])]
    width = RANK * RANK
    step = 128
    for at in range(0, width, step):
        source, target = iota((step, width), 0) + at, iota((step, width), 1)
        turned = ((target & (RANK - 1)) << 5) + (target >> 5)
        flip_ref[at : at + step] = jnp.where(source == turned, 1.0, 0.0).astype(bf16)
    half = pl.ds(pl.multiple_of(core_ref[0] * HALF, HALF), HALF)
    total = jnp.zeros((RANK, LOADS), f32)
    for copy in copies:
        copy.wait()
    for j in range(3):
        total += dot32(bases[0, j], dens[0, j])
        own_ref[j * HALF : (j + 1) * HALF] = jnp.transpose(dens[0, j, half, :])
    moments_ref[...] = total.astype(bf16)


def in_hbm(array):
    return pltpu.with_memory_space_constraint(array, pltpu.HBM)


def moments_of(core, densities, bases):
    width = RANK * RANK
    return pl.pallas_call(
        moments_kernel,
        out_shape=(
            jax.ShapeDtypeStruct((DENS, LOADS), bf16),
            jax.ShapeDtypeStruct((RANK, LOADS), bf16),
            jax.ShapeDtypeStruct((width, width), bf16),
        ),
        in_specs=[pl.BlockSpec(memory_space=pltpu.SMEM)] + [pl.BlockSpec(memory_space=pltpu.HBM)] * 2,
        out_specs=tuple(whole(3)),
        scratch_shapes=[
            pltpu.VMEM(densities.shape, bf16),
            pltpu.VMEM(bases.shape, bf16),
            pltpu.SemaphoreType.DMA((2,)),
        ],
        compiler_params=pltpu.CompilerParams(vmem_limit_bytes=VMEM_LIMIT),
        name="moments",
    )(jnp.reshape(core, (1,)), in_hbm(densities), in_hbm(bases))


def unit_kernel(core_ref, own_ref, partner_ref, moments_ref, unit_ref):
    half = pl.ds(pl.multiple_of(core_ref[0] * HALF, HALF), HALF)
    unit_ref[:DENS] = own_ref[...]
    for j in range(3):
        unit_ref[DENS + j * HALF : DENS + (j + 1) * HALF] = jnp.transpose(
            partner_ref[0, j, half, :]
        )
    unit_ref[2 * DENS :] = moments_ref[...]


def make_unit(core, own, partner, moments):
    return pl.pallas_call(
        unit_kernel,
        out_shape=jax.ShapeDtypeStruct((UNIT, LOADS), bf16),
        in_specs=[pl.BlockSpec(memory_space=pltpu.SMEM)] + whole(3),
        out_specs=whole(1)[0],
        compiler_params=pltpu.CompilerParams(vmem_limit_bytes=VMEM_LIMIT),
        name="unit",
    )(jnp.reshape(core, (1,)), own, partner, moments)


def points_kernel(
    here_ref, positions_ref, areas_ref, couplings_ref,
    spread_ref, targets_ref, held_couplings, columns, positions, areas, sems,
):
    first = [fetch(positions_ref, positions, sems.at[0]), fetch(areas_ref, areas, sems.at[1])]
    last = fetch(couplings_ref, held_couplings, sems.at[2])
    z, core, y, x = (here_ref[k] for k in range(4))
    half = lambda whole_row: jnp.where(core == 0, whole_row[:, :HALF], whole_row[:, HALF:])
    back = (0, 3, 1, 2)
    for copy in first:
        copy.wait()
    for t, (step, other) in enumerate(TARGETS):
        cluster = ((step + z) & 3) * 32 + ((other + core) & 1) * 16 + y * SIDE + x
        for i in range(3):
            targets_ref[t, i : i + 1, :] = positions[i, pl.ds(cluster, 1), :]
        targets_ref[t, 3:4, :] = areas[pl.ds(cluster, 1), :]
    for s in range(32):
        first, second = back[(s >> 1) & 3], back[s >> 3]
        on_x = (x + jnp.where(core == 0, first, second)) & 3
        on_y = (y + jnp.where(core == 0, second, first)) & 3
        cluster = z * 32 + ((s + core) & 1) * 16 + on_y * SIDE + on_x
        for i in range(3):
            columns[s, i : i + 1, :] = half(positions[i, pl.ds(cluster, 1), :])
        columns[s, 3:4, :] = half(areas[pl.ds(cluster, 1), :])
    for s in range(32):
        upright = jnp.transpose(columns[s])
        for i in range(4):
            spread_ref[s, i] = jnp.broadcast_to(upright[:, i : i + 1], (HALF, LOADS))
    last.wait()


def make_points(here, positions, areas, couplings):
    return pl.pallas_call(
        points_kernel,
        out_shape=(
            jax.ShapeDtypeStruct((32, 4, HALF, LOADS), f32),
            jax.ShapeDtypeStruct((8, 8, CS), f32),
            jax.ShapeDtypeStruct(couplings.shape, bf16),
        ),
        in_specs=[pl.BlockSpec(memory_space=pltpu.SMEM)] + [pl.BlockSpec(memory_space=pltpu.HBM)] * 3,
        out_specs=tuple(whole(3)),
        scratch_shapes=[
            pltpu.VMEM((32, 8, HALF), f32),
            pltpu.VMEM(positions.shape, f32),
            pltpu.VMEM(areas.shape, f32),
            pltpu.SemaphoreType.DMA((3,)),
        ],
        compiler_params=pltpu.CompilerParams(vmem_limit_bytes=VMEM_LIMIT),
        name="points",
    )(here, in_hbm(positions), in_hbm(areas), in_hbm(couplings))


def blocks_kernel(forward_ref, backward_ref, couplings_ref, flip_ref, blocks_ref):
    cells = 128
    far = couplings_ref.shape[0]

    def summed(cell_ref):
        marks = iota((cells, far), 0) == cell_ref[...]
        return dot32(jnp.where(marks, 1.0, 0.0).astype(bf16), couplings_ref[...])

    total = summed(forward_ref) + dot32(summed(backward_ref).astype(bf16), flip_ref[...])
    for u in range(16):
        unit = total[u * 8 : (u + 1) * 8]
        for g in range(0, 8, 2):
            two = [unit[:, k * 128 : (k + 1) * 128] for k in (g, g + 1)]
            lanes = slice(u * 128, (u + 1) * 128)
            blocks_ref[g * 8 : (g + 2) * 8, lanes] = jnp.concatenate(two, axis=0).astype(bf16)


def make_blocks(forward, backward, couplings, flip):
    return pl.pallas_call(
        blocks_kernel,
        out_shape=jax.ShapeDtypeStruct((64, 16 * 128), bf16),
        in_specs=whole(4),
        out_specs=whole(1)[0],
        compiler_params=pltpu.CompilerParams(vmem_limit_bytes=VMEM_LIMIT),
        name="coupling_blocks",
    )(forward[None, :], backward[None, :], couplings, flip)


def near_kernel(first_unit, buffers, part, counts, targets, spread, *refs):
    units = 2 * buffers
    slots = 2 * units
    held, refs = refs[:buffers], refs[buffers:]
    low, high = SPANS[part]
    sums_far = part in ("first", "middle", "send")
    if sums_far:
        blocks, refs = refs[0], refs[1:]
    if part in ("middle", "send"):
        carried, carried_far, refs = refs[0], refs[1], refs[2:]
    elif part == "keep":
        carried, far, refs = refs[0], refs[1], refs[2:]
    elif part == "own":
        far, refs = refs[0], refs[1:]
    if part == "send":
        send, far, acc, refs = refs[0], refs[1], refs[2], refs[3:]
    elif sums_far:
        acc, far, refs = refs[0], refs[1], refs[2:]
    elif part == "keep":
        acc, refs = refs[0], refs[1:]
    else:
        acc, pair, refs = refs[0], refs[1], refs[2:]
    flat, tile_a, tile_b, entry = refs[:4]

    for k in range(buffers):
        flat[k * 2 * UNIT : (k + 1) * 2 * UNIT] = held[k][...]

    def list_target(t, filled):
        for value in [counts[t, 2 * first_unit + s] for s in range(slots)]:
            entry[filled] = value
            filled = filled + jnp.where(value >= 4096, 1, 0)
        entry[filled] = t * 64 + 2 * first_unit
        return filled + (filled & 1)

    entries = lax.fori_loop(low, high, list_target, 0)
    for k in range(6):
        entry[entries + k] = low * 64 + 2 * first_unit
    near_rows = slice(0, 3 * CS)
    if part in ("first", "own"):
        acc[:, near_rows] = jnp.zeros((high - low, 3 * CS, LOADS), f32)
    else:
        acc[:, near_rows] = carried[low:high]

    if sums_far:
        wide = refs[4]
        wide[...] = jnp.zeros(wide.shape, bf16)
        for u in range(units):
            moments = flat[u * UNIT + 2 * DENS : (u + 1) * UNIT, :]
            for k in range(4):
                at = u * 128 + k * RANK
                wide[at : at + RANK, k * LOADS : (k + 1) * LOADS] = moments
        coefficients = dot32(blocks[...], wide[...])
        for k in range(4):
            piece = coefficients[:, k * LOADS : (k + 1) * LOADS]
            far[k] = piece if part == "first" else carried_far[k] + piece

    def coefficients_of(t):
        return jnp.concatenate([far[k, pl.ds(t, 8, stride=8), :] for k in range(4)], axis=0)

    def decode(k):
        both = [entry[2 * k + h] for h in range(2)]
        return (both[0] >> 6) & 7, [v & 63 for v in both], [v >> 12 for v in both]

    def make_tile(k, tile):
        t, slot, pairs = decode(k)
        amount = [p.astype(f32) * kelvin_coef for p in pairs]
        point = targets[t]
        step = 16
        for at in range(0, CS, step):
            side = at // HALF
            rows = slice(at % HALF, at % HALF + step)
            here = [spread[slot[side], i, rows] for i in range(4)]
            for h in range(2):
                lanes = slice(h * HALF, (h + 1) * HALF)
                dx, dy, dz = (here[i] - point[i : i + 1, lanes] for i in range(3))
                inverse = lax.rsqrt(dx * dx + dy * dy + dz * dz + eps_square)
                scaled = (here[3] * (point[3:4, lanes] * amount[side])) * inverse
                cubed = scaled * (inverse * inverse)
                level = lame_ratio * scaled
                ex, ey, ez = dx * cubed, dy * cubed, dz * cubed
                values = (dx * ex + level, dy * ey + level, dz * ez + level, dx * ey, dx * ez, dy * ez)
                for b in range(6):
                    tile[b, at : at + step, lanes] = values[b].astype(bf16)

    def add_products(k, tile):
        t, slot, _ = decode(k)
        f = []
        for j in range(3):
            parts = []
            for h in range(2):
                base = ((slot[h] >> 1) - first_unit) * UNIT + (slot[h] & 1) * DENS + j * HALF
                parts.append(flat[pl.ds(pl.multiple_of(base, 16), HALF), :])
            f.append(jnp.concatenate(parts, axis=1))
        f = jnp.concatenate(f, axis=1)
        order = ((0, 3, 4), (3, 1, 5), (4, 5, 2))
        sums = [
            dot32(f, jnp.concatenate([tile[b] for b in order[i]], axis=0)) for i in range(3)
        ]
        for i in range(3):
            for h in range(2):
                at = (2 * i + h) * HALF
                acc[t - low, at : at + HALF] += sums[i][:, h * HALF : (h + 1) * HALF]

    tasks = entries >> 1

    @pl.when(tasks > 0)
    def _():
        make_tile(0, tile_a)

        def two_tasks(k, carry):
            make_tile(2 * k + 1, tile_b)
            add_products(2 * k, tile_a)

            @pl.when(2 * k + 1 < tasks)
            def _():
                make_tile(2 * k + 2, tile_a)
                add_products(2 * k + 1, tile_b)

            return carry

        lax.fori_loop(0, (tasks + 1) >> 1, two_tasks, 0)

    if part == "send":
        for t in range(low, high):
            send[t - low, : 3 * CS] = acc[t - low].astype(bf16)
            send[t - low, 3 * CS :] = coefficients_of(t).astype(bf16)
    elif not sums_far:
        for t in range(low, high):
            acc[t - low, 3 * CS :] = coefficients_of(t)
    if part == "own":
        for k in range(2):
            pair[k] = acc[1].astype(bf16)


def near(part, first_unit, buffers, carried, counts, targets, spread, blocks):
    count = len(buffers)
    slots = 4 * count
    sums = jax.ShapeDtypeStruct((AWAY, 3 * CS, LOADS), f32)
    far = jax.ShapeDtypeStruct((4, 64, LOADS), f32)
    scratch = [
        pltpu.VMEM((count * 2 * UNIT, LOADS), bf16),
        pltpu.VMEM((6, CS, CS), bf16),
        pltpu.VMEM((6, CS, CS), bf16),
        pltpu.SMEM((8 * slots + 16,), jnp.int32),
    ]
    operands = [counts, targets, spread, *buffers]
    low, high = SPANS[part]
    if part in ("keep", "own"):
        shapes = (jax.ShapeDtypeStruct((high - low, FULL, LOADS), f32),)
        if part == "own":
            shapes += (jax.ShapeDtypeStruct((2, FULL, LOADS), bf16),)
    else:
        operands.append(blocks[:, first_unit * 128 : (first_unit + 2 * count) * 128])
        scratch.append(pltpu.VMEM((2 * count * 128, 4 * LOADS), bf16))
        shapes = (sums, far)
        if part == "send":
            shapes = (jax.ShapeDtypeStruct((high - low, FULL, LOADS), bf16), far)
            scratch = [pltpu.VMEM((high - low, 3 * CS, LOADS), f32)] + scratch
    operands += carried
    return pl.pallas_call(
        functools.partial(near_kernel, first_unit, count, part),
        out_shape=shapes,
        in_specs=[pl.BlockSpec(memory_space=pltpu.SMEM)] + whole(len(operands) - 1),
        out_specs=tuple(whole(len(shapes))),
        scratch_shapes=scratch,
        compiler_params=pltpu.CompilerParams(vmem_limit_bytes=VMEM_LIMIT),
        cost_estimate=pl.CostEstimate(
            flops=count * 1_000_000_000, bytes_accessed=8_000_000, transcendentals=count * 500_000
        ),
        name=f"near_{part}",
    )(*operands)


def finish_kernel(core, keep, swapped, one, two, three, bases, out):
    def total(rows):
        return (
            keep[0, rows] + swapped[1 - core[0], rows].astype(f32) + one[rows].astype(f32)
            + two[rows].astype(f32) + three[rows].astype(f32)
        )

    coefficients = total(slice(3 * CS, FULL))
    high = coefficients.astype(bf16)
    low = (coefficients - high.astype(f32)).astype(bf16)
    both = jnp.concatenate([high, low], axis=0)
    row, held = iota((2 * RANK, 2 * RANK), 0), iota((2 * RANK, 2 * RANK), 1)
    from_row = (row & 32) + ((row & 3) << 3) + ((row & 31) >> 2)
    order = jnp.where(held == from_row, 1.0, 0.0).astype(bf16)
    both = dot32(order, both).astype(bf16)
    for j in range(3):
        basis = bases[0, j]
        twice = jnp.concatenate([basis, basis], axis=0)
        expanded = lax.dot_general(
            twice, both, (((0,), (0,)), ((), ())), preferred_element_type=f32
        )
        for h in range(2):
            at = (2 * j + h) * HALF
            near_part = jnp.transpose(total(slice(at, at + HALF)))
            panels = slice(h * HALF, (h + 1) * HALF)
            out[0, j, panels] = (near_part + expanded[panels]).astype(bf16)


def finish(core, keep, swapped, others, bases):
    return pl.pallas_call(
        finish_kernel,
        out_shape=jax.ShapeDtypeStruct((1, 3, CS, LOADS), bf16),
        in_specs=[pl.BlockSpec(memory_space=pltpu.SMEM)] + whole(6),
        out_specs=whole(1)[0],
        compiler_params=pltpu.CompilerParams(vmem_limit_bytes=VMEM_LIMIT),
        name="sum_and_expand",
    )(jnp.reshape(core, (1,)), keep, swapped, *others, bases)


def local(densities, positions, areas, bases, near_pairs, far_pairs, couplings):
    row = lax.axis_index("row")
    col = lax.axis_index("col")
    z, core = row >> 1, row & 1
    y, x = col >> 2, col & 3
    first_at = jnp.where(core == 0, x, y)
    second_at = jnp.where(core == 0, y, x)

    def unit_of(cluster):
        on_y, on_x = (cluster >> 2) & 3, cluster & 3
        first = (jnp.where(core == 0, on_x, on_y) - first_at) & 3
        second = (jnp.where(core == 0, on_y, on_x) - second_at) & 3
        put = lambda r: jnp.where(r == 0, 0, jnp.where(r == 1, 2, jnp.where(r == 2, 3, 1)))
        return put(second) * SIDE + put(first)

    def other_core(cluster):
        return ((cluster >> 4) + core) & 1

    def slot_of(cluster):
        return jnp.where(cluster >> 5 == z, unit_of(cluster) * 2 + other_core(cluster), -1)

    def target_of(cluster):
        step, other = ((cluster >> 5) - z) & 3, other_core(cluster)
        place = jnp.where(step == 0, AWAY + other, other * 3 + step - 1)
        return jnp.where((cluster & 15) == col, place, -1)

    bases = jnp.transpose(bases, (0, 2, 1, 3))
    positions = jnp.transpose(positions, (1, 0, 2))

    partner = swap_core(densities)
    own, moments, flip = moments_of(core, densities, bases)
    unit = make_unit(core, own, partner, moments)
    from_below = along_first(unit, 1)
    from_above = along_first(unit, -1)
    from_across = along_first(unit, 2)
    here = jnp.stack([z, core, y, x]).astype(jnp.int32)
    here, unit = lax.optimization_barrier((here, unit))
    spread, targets, couplings = make_points(here, positions, areas, couplings)
    (near_pairs, far_pairs, couplings, spread, targets, unit, from_below, from_above, from_across) = (
        lax.optimization_barrier(
            (near_pairs, far_pairs, couplings, spread, targets, unit)
            + (from_below, from_above, from_across)
        )
    )
    low = jnp.concatenate([unit, from_below], axis=0)
    high = jnp.concatenate([from_above, from_across], axis=0)
    low_below = along_second(low, 1)
    high_above = along_second(high, -1)

    heads, tails = near_pairs[:, 0], near_pairs[:, 1]
    mark = lambda index, size: index[None, :] == jnp.arange(size, dtype=jnp.int32)[:, None]
    to_targets = jnp.concatenate(
        [target_of(heads), jnp.where(heads != tails, target_of(tails), -1)]
    )
    from_slots = jnp.concatenate([slot_of(tails), slot_of(heads)])
    counts = lax.dot_general(
        mark(to_targets, 8).astype(bf16),
        mark(from_slots, 32).astype(bf16),
        (((1,), (1,)), ((), ())),
        preferred_element_type=f32,
    ).astype(jnp.int32)
    counts = counts * 4096 + jnp.arange(8, dtype=jnp.int32)[:, None] * 64 + jnp.arange(32, dtype=jnp.int32)

    far_heads, far_tails = far_pairs[:, 0], far_pairs[:, 1]

    def cell(target, source):
        ours = (target_of(target) >= 0) & (slot_of(source) >= 0) & (other_core(source) == 0)
        return jnp.where(ours, unit_of(source) * 8 + target_of(target), -1)

    back_cell = jnp.where(far_heads != far_tails, cell(far_tails, far_heads), -1)
    blocks = make_blocks(cell(far_heads, far_tails), back_cell, couplings, flip)
    blocks, low_later, high_later = lax.optimization_barrier((blocks, low, high))
    high_below = along_second(high_later, 1)
    low_above = along_second(low_later, -1)
    tables = (counts, targets, spread)

    carried = near("first", 0, (low, high), (), *tables, blocks)
    low_below, high_above, carried = lax.optimization_barrier((low_below, high_above, carried))
    low_across = along_second(low_below, 1)
    high_across = along_second(high_above, -1)
    beside = (low_below, high_below, low_above, high_above)
    carried = near("middle", 4, beside, carried, *tables, blocks)
    across = (low_across, high_across)
    send, far = near("send", 12, across, carried, *tables, blocks)
    swapped = swap_core(send)
    (keep,) = near("keep", 12, across, (carried[0], far), *tables, blocks)
    both = [(keep[k] + swapped[k].astype(f32)).astype(bf16) for k in range(3)]
    both, far = lax.optimization_barrier((both, far))
    others = [along_z(both[0], 1), along_z(both[2], 3)]
    others.append(along_z(both[1], 2))
    everything = (low, high) + beside + across
    own, pair = near("own", 0, everything, (far,), *tables, blocks)
    chips = [[2 * k, 2 * k + 1] for k in range(SIDE)]
    swapped = lax.all_to_all(pair, "row", 0, 0, axis_index_groups=chips, tiled=True)
    return finish(core, own, swapped, others, bases)


def solution(mesh):
    return jax.shard_map(
        local,
        mesh=mesh,
        in_specs=(
            P(("row", "col"), None, None, None),
            P(),
            P(),
            P(("row", "col"), None, None, None),
            P(),
            P(),
            P(),
        ),
        out_specs=P(("row", "col"), None, None, None),
        check_vma=False,
    )
```

profile of v0, /device:TPU:1, one launch (start us, length us, event | category | flops | bytes accessed | tf_op | source)
XLA Modules:
  0.0 60.3 jit_solution(16608648241612911379)
XLA Ops:
  0.0 1.4 %collective-permute-start = (bf16[1,3,256,128]{3,2,1,0:T(8,128)(2,1)}, bf16[1,3,256,128]{3,2,1,0:T(8,128)(2,1)S(1)}, u32[]{:S(2)}, u32[]{:S(2)}) collective-permute-start(bf16[1,3,256,128]{3,2,1,0:T(8,128)(2,1)} %dens_ref.1), channel_id=1, source_target_pairs={{0,16},{1,17},{2,18},{3,19},{4,20},{5,21},{6,22},{7,23},{8,24},{9,... | collective-permute-start | bytes 589832 | tf_op jit(solution)/shard_map/ppermute | solution.py:46
  1.4 1.1 %moments.1 = (bf16[384,128]{1,0:T(8,128)(2,1)S(1)}, bf16[32,128]{1,0:T(8,128)(2,1)S(1)}, bf16[1024,1024]{1,0:T(8,128)(2,1)S(1)}) custom-call(s32[1]{0:T(128)} %bitcast.core_ref.core, bf16[1,3,256,128]{3,2,1,0:T(8,128)(2,1)} %dens_ref.1, bf16[1,3,32,256]{3,2,1,0:T(8,128)(2,1)} %bitcast.68), custom_call_target="tpu_custom_call" | custom-call | tf_op jit(solution)/shard_map/moments/pallas_call | solution.py:105
  2.5 0.2 collective-permute-done.partner_ref
  2.7 0.1 unit.1
  2.8 3.1 %collective-permute-start.3 = (bf16[800,128]{1,0:T(8,128)(2,1)S(1)}, bf16[800,128]{1,0:T(8,128)(2,1)S(1)}, u32[]{:S(2)}, u32[]{:S(2)}) collective-permute-start(bf16[800,128]{1,0:T(8,128)(2,1)S(1)} %unit.1), channel_id=1, source_target_pairs={{0,2},{1,3},{2,0},{3,1},{4,6},{5,7},{6,4},{7,5},{8,10},{9,11},{10,... | collective-permute-start | bytes 614408 | tf_op jit(solution)/shard_map/ppermute | solution.py:51
  5.9 0.8 %collective-permute-start.2 = (bf16[800,128]{1,0:T(8,128)(2,1)S(1)}, bf16[800,128]{1,0:T(8,128)(2,1)S(1)}, u32[]{:S(2)}, u32[]{:S(2)}) collective-permute-start(bf16[800,128]{1,0:T(8,128)(2,1)S(1)} %unit.1), channel_id=1, source_target_pairs={{0,3},{1,0},{2,1},{3,2},{4,7},{5,4},{6,5},{7,6},{8,11},{9,8},{10,9... | collective-permute-start | bytes 614408 | tf_op jit(solution)/shard_map/ppermute | solution.py:51
  6.7 0.7 %collective-permute-start.1 = (bf16[800,128]{1,0:T(8,128)(2,1)S(1)}, bf16[800,128]{1,0:T(8,128)(2,1)S(1)}, u32[]{:S(2)}, u32[]{:S(2)}) collective-permute-start(bf16[800,128]{1,0:T(8,128)(2,1)S(1)} %unit.1), channel_id=1, source_target_pairs={{0,1},{1,2},{2,3},{3,0},{4,5},{5,6},{6,7},{7,4},{8,9},{9,10},{10,1... | collective-permute-start | bytes 614408 | tf_op jit(solution)/shard_map/ppermute | solution.py:51
  7.3 0.1 pad_add_fusion.2.here_ref
  7.4 4.6 %points.1 = (f32[32,4,128,128]{3,2,1,0:T(8,128)S(1)}, f32[8,8,256]{2,1,0:T(8,128)S(1)}, bf16[768,1024]{1,0:T(8,128)(2,1)S(1)}) custom-call(s32[4]{0:T(128)S(1)} %pad_add_fusion.2.here_ref, f32[3,128,256]{2,1,0:T(8,128)} %bitcast.70, f32[128,256]{1,0:T(8,128)} %areas_ref.1, bf16[768,1024]{1,0:T(8,128)(2,1)} %couplings_ref.1), custom_call_target="tpu_custom_call" | custom-call | tf_op jit(solution)/shard_map/points/pallas_call | solution.py:177
  12.0 0.0 collective-permute-done.3
  12.0 0.0 collective-permute-done.2
  12.1 0.7 %collective-permute-done.1 = bf16[800,128]{1,0:T(8,128)(2,1)S(1)} collective-permute-done((bf16[800,128]{1,0:T(8,128)(2,1)S(1)}, bf16[800,128]{1,0:T(8,128)(2,1)S(1)}, u32[]{:S(2)}, u32[]{:S(2)}) %collective-permute-start.1) | collective-permute-done | bytes 204832 | tf_op jit(solution)/shard_map/ppermute | solution.py:51
  12.8 0.0 copy-done.1
  12.8 0.1 compare_reduce_fusion.2
  12.9 0.2 fusion.27
  13.1 0.0 copy-done.2
  13.1 0.1 bitcast_select_fusion.1
  13.3 2.3 %collective-permute-start.5 = (bf16[1600,128]{1,0:T(8,128)(2,1)S(1)}, bf16[1600,128]{1,0:T(8,128)(2,1)S(1)}, u32[]{:S(2)}, u32[]{:S(2)}) collective-permute-start(bf16[1600,128]{1,0:T(8,128)(2,1)S(1)} %constant_dynamic-update-slice_fusion.2.refs_1_), channel_id=1, source_target_pairs={{0,12},{1,13},{2,14},{3,15},{4,0},{5,1},{6,2},{7,3},{8,4},{9,5},{1... | collective-permute-start | bytes 1228808 | tf_op jit(solution)/shard_map/ppermute | solution.py:56
  15.6 0.1 collective-permute-start.4
  15.6 0.9 %coupling_blocks.1 = bf16[64,2048]{1,0:T(8,128)(2,1)S(1)} custom-call(s32[1,768]{1,0:T(1,128)S(1)} %get-tuple-element.90.forward_ref, s32[1,768]{1,0:T(1,128)S(1)} %get-tuple-element.89.backward_ref, bf16[768,1024]{1,0:T(8,128)(2,1)S(1)} %get-tuple-element.56.couplings_ref, bf16[1024,1024]{1,0:T(8,128)(2,1)S(1)} %get-tuple-element.57.flip_ref), custom_call_target="tpu_custom_call" | custom-call | tf_op jit(solution)/shard_map/coupling_blocks/pallas_call | solution.py:215
  16.6 0.2 collective-permute-start.6
  16.8 2.6 %collective-permute-start.7 = (bf16[1600,128]{1,0:T(8,128)(2,1)S(1)}, bf16[1600,128]{1,0:T(8,128)(2,1)S(1)}, u32[]{:S(2)}, u32[]{:S(2)}) collective-permute-start(bf16[1600,128]{1,0:T(8,128)(2,1)S(1)} %constant_dynamic-update-slice_fusion.refs_0_), channel_id=1, source_target_pairs={{0,12},{1,13},{2,14},{3,15},{4,0},{5,1},{6,2},{7,3},{8,4},{9,5},{1... | collective-permute-start | bytes 1228808 | tf_op jit(solution)/shard_map/ppermute | solution.py:56
  19.4 0.2 fusion.2.counts
  19.6 4.0 %near_first.1 = (f32[6,768,128]{2,1,0:T(8,128)S(1)}, f32[4,64,128]{2,1,0:T(8,128)S(1)}) custom-call(s32[8,32]{1,0:T(8,128)S(1)} %fusion.2.counts, f32[8,8,256]{2,1,0:T(8,128)S(1)} %get-tuple-element.49.targets, f32[32,4,128,128]{3,2,1,0:T(8,128)S(1)} %get-tuple-element.50.spread, bf16[1600,128]{1,0:T(8,128)(2,1)S(1)} %constant_dynamic-update-slice_fusion.refs_0_, ...), custom_call_target="tpu_custom_call" | custom-call | flops 2000000000 | bytes 8000000 | tf_op jit(solution)/shard_map/near_first/pallas_call | solution.py:384
  23.6 0.0 collective-permute-done.5.refs_3_.refs_5_
  23.6 0.3 collective-permute-done.4.refs_0_.refs_2_
  23.9 0.0 collective-permute-start.8
  23.9 2.7 %collective-permute-start.9 = (bf16[1600,128]{1,0:T(8,128)(2,1)S(1)}, bf16[1600,128]{1,0:T(8,128)(2,1)S(1)}, u32[]{:S(2)}, u32[]{:S(2)}) collective-permute-start(bf16[1600,128]{1,0:T(8,128)(2,1)S(1)} %collective-permute-done.5.refs_3_.refs_5_), channel_id=1, source_target_pairs={{0,12},{1,13},{2,14},{3,15},{4,0},{5,1},{6,2},{7,3},{8,4},{9,5},{1... | collective-permute-start | bytes 1228808 | tf_op jit(solution)/shard_map/ppermute | solution.py:56
  26.6 1.7 %collective-permute-done.6.refs_1_.refs_3_ = bf16[1600,128]{1,0:T(8,128)(2,1)S(1)} collective-permute-done((bf16[1600,128]{1,0:T(8,128)(2,1)S(1)}, bf16[1600,128]{1,0:T(8,128)(2,1)S(1)}, u32[]{:S(2)}, u32[]{:S(2)}) %collective-permute-start.6) | collective-permute-done | bytes 409632 | tf_op jit(solution)/shard_map/ppermute | solution.py:56
  28.3 0.0 collective-permute-done.7.refs_2_.refs_4_
  28.3 5.7 %near_middle.1 = (f32[6,768,128]{2,1,0:T(8,128)S(1)}, f32[4,64,128]{2,1,0:T(8,128)S(1)}) custom-call(s32[8,32]{1,0:T(8,128)S(1)} %fusion.2.counts, f32[8,8,256]{2,1,0:T(8,128)S(1)} %get-tuple-element.49.targets, f32[32,4,128,128]{3,2,1,0:T(8,128)S(1)} %get-tuple-element.50.spread, bf16[1600,128]{1,0:T(8,128)(2,1)S(1)} %collective-permute-done.4.refs_0_.refs_2_, ...), custom_call_target="tpu_custom_call" | custom-call | flops 4000000000 | bytes 8000000 | tf_op jit(solution)/shard_map/near_middle/pallas_call | solution.py:384
  34.1 0.0 collective-permute-done.8.refs_0_.refs_6_
  34.1 0.0 collective-permute-done.9.refs_1_.refs_7_
  34.1 2.8 %near_send.1 = (bf16[3,800,128]{2,1,0:T(8,128)(2,1)S(1)}, f32[4,64,128]{2,1,0:T(8,128)S(1)}) custom-call(s32[8,32]{1,0:T(8,128)S(1)} %fusion.2.counts, f32[8,8,256]{2,1,0:T(8,128)S(1)} %get-tuple-element.49.targets, f32[32,4,128,128]{3,2,1,0:T(8,128)S(1)} %get-tuple-element.50.spread, bf16[1600,128]{1,0:T(8,128)(2,1)S(1)} %collective-permute-done.8.refs_0_.refs_6_, ...), custom_call_target="tpu_custom_call" | custom-call | flops 2000000000 | bytes 8000000 | tf_op jit(solution)/shard_map/near_send/pallas_call | solution.py:384
  36.9 2.7 %collective-permute-start.10 = (bf16[3,800,128]{2,1,0:T(8,128)(2,1)S(1)}, bf16[3,800,128]{2,1,0:T(8,128)(2,1)S(1)}, u32[]{:S(2)}, u32[]{:S(2)}) collective-permute-start(bf16[3,800,128]{2,1,0:T(8,128)(2,1)S(1)} %get-tuple-element.70), channel_id=1, source_target_pairs={{0,16},{1,17},{2,18},{3,19},{4,20},{5,21},{6,22},{7,23},{8,24},{9,... | collective-permute-start | bytes 1843208 | tf_op jit(solution)/shard_map/ppermute | solution.py:46
  39.6 1.9 %near_keep.1 = f32[3,800,128]{2,1,0:T(8,128)S(1)} custom-call(s32[8,32]{1,0:T(8,128)S(1)} %fusion.2.counts, f32[8,8,256]{2,1,0:T(8,128)S(1)} %get-tuple-element.49.targets, f32[32,4,128,128]{3,2,1,0:T(8,128)S(1)} %get-tuple-element.50.spread, bf16[1600,128]{1,0:T(8,128)(2,1)S(1)} %collective-permute-done.8.refs_0_.refs_6_, ...), custom_call_target="tpu_custom_call" | custom-call | flops 2000000000 | bytes 8000000 | tf_op jit(solution)/shard_map/near_keep/pallas_call | solution.py:384
  41.5 0.0 collective-permute-done.10
  41.5 0.2 fusion.9
  41.7 0.0 copy-start
  41.7 3.0 %collective-permute-start.11 = (bf16[800,128]{1,0:T(8,128)(2,1)S(1)}, bf16[800,128]{1,0:T(8,128)(2,1)S(1)}, u32[]{:S(2)}, u32[]{:S(2)}) collective-permute-start(bf16[800,128]{1,0:T(8,128)(2,1)S(1)} %get-tuple-element.74), channel_id=1, source_target_pairs={{0,32},{1,33},{2,34},{3,35},{4,36},{5,37},{6,38},{7,39},{8,40},{9,... | collective-permute-start | bytes 614408 | tf_op jit(solution)/shard_map/ppermute | solution.py:60
  44.6 3.3 %collective-permute-start.12 = (bf16[800,128]{1,0:T(8,128)(2,1)S(1)}, bf16[800,128]{1,0:T(8,128)(2,1)S(1)}, u32[]{:S(2)}, u32[]{:S(2)}) collective-permute-start(bf16[800,128]{1,0:T(8,128)(2,1)S(1)} %get-tuple-element.75), channel_id=1, source_target_pairs={{0,96},{1,97},{2,98},{3,99},{4,100},{5,101},{6,102},{7,103},{8,104... | collective-permute-start | bytes 614408 | tf_op jit(solution)/shard_map/ppermute | solution.py:60
  48.0 1.3 %collective-permute-start.13 = (bf16[800,128]{1,0:T(8,128)(2,1)S(1)}, bf16[800,128]{1,0:T(8,128)(2,1)S(1)}, u32[]{:S(2)}, u32[]{:S(2)}) collective-permute-start(bf16[800,128]{1,0:T(8,128)(2,1)S(1)} %get-tuple-element.76), channel_id=1, source_target_pairs={{0,64},{1,65},{2,66},{3,67},{4,68},{5,69},{6,70},{7,71},{8,72},{9,... | collective-permute-start | bytes 614408 | tf_op jit(solution)/shard_map/ppermute | solution.py:60
  49.2 5.4 %near_own.1 = (f32[2,800,128]{2,1,0:T(8,128)S(1)}, bf16[2,800,128]{2,1,0:T(8,128)(2,1)S(1)}) custom-call(s32[8,32]{1,0:T(8,128)S(1)} %fusion.2.counts, f32[8,8,256]{2,1,0:T(8,128)S(1)} %get-tuple-element.49.targets, f32[32,4,128,128]{3,2,1,0:T(8,128)S(1)} %get-tuple-element.50.spread, bf16[1600,128]{1,0:T(8,128)(2,1)S(1)} %constant_dynamic-update-slice_fusion.refs_0_, ...), custom_call_target="tpu_custom_call" | custom-call | flops 8000000000 | bytes 8000000 | tf_op jit(solution)/shard_map/near_own/pallas_call | solution.py:384
  54.7 4.6 %all_to_all.5.swapped = bf16[2,800,128]{2,1,0:T(8,128)(2,1)S(1)} all-to-all(bf16[2,800,128]{2,1,0:T(8,128)(2,1)S(1)} %get-tuple-element.73), channel_id=1, replica_groups={{0,16},{32,48},{64,80},{96,112},{1,17},{33,49},{65,81},{97,113},{2,18},..., dimensions={0} | all-to-all | bytes 819200 | tf_op jit(solution)/shard_map/all_to_all | solution.py:530
  59.3 0.0 collective-permute-done.11.one
  59.3 0.0 collective-permute-done.12.two
  59.3 0.0 collective-permute-done.13.three
  59.3 1.0 %sum_and_expand.1 = bf16[1,3,256,128]{3,2,1,0:T(8,128)(2,1)} custom-call(s32[1]{0:T(128)} %bitcast.core_ref.core, f32[2,800,128]{2,1,0:T(8,128)S(1)} %get-tuple-element.72.keep, bf16[2,800,128]{2,1,0:T(8,128)(2,1)S(1)} %all_to_all.5.swapped, bf16[800,128]{1,0:T(8,128)(2,1)S(1)} %collective-permute-done.11.one, ...), custom_call_target="tpu_custom_call" | custom-call | tf_op jit(solution)/shard_map/sum_and_expand/pallas_call | solution.py:427
  (13 shorter events, 0.1 us)
Async XLA Ops:
  0.0 13.1 %copy-start.2 = (s32[768,2]{0,1:T(2,128)S(1)}, s32[768,2]{0,1:T(2,128)}, u32[]{:S(2)}) copy-start(s32[768,2]{0,1:T(2,128)} %param.12) | copy-start | bytes 18436
  0.0 12.8 %copy-start.1 = (s32[1920,2]{0,1:T(2,128)S(1)}, s32[1920,2]{0,1:T(2,128)}, u32[]{:S(2)}) copy-start(s32[1920,2]{0,1:T(2,128)} %param.11) | copy-start | bytes 46084
  0.0 2.7 %collective-permute-start = (bf16[1,3,256,128]{3,2,1,0:T(8,128)(2,1)}, bf16[1,3,256,128]{3,2,1,0:T(8,128)(2,1)S(1)}, u32[]{:S(2)}, u32[]{:S(2)}) collective-permute-start(bf16[1,3,256,128]{3,2,1,0:T(8,128)(2,1)} %dens_ref.1), channel_id=1, source_target_pairs={{0,16},{1,17},{2,18},{3,19},{4,20},{5,21},{6,22},{7,23},{8,24},{9,... | collective-permute-start | bytes 589832 | tf_op jit(solution)/shard_map/ppermute | solution.py:46
  2.8 9.2 %collective-permute-start.3 = (bf16[800,128]{1,0:T(8,128)(2,1)S(1)}, bf16[800,128]{1,0:T(8,128)(2,1)S(1)}, u32[]{:S(2)}, u32[]{:S(2)}) collective-permute-start(bf16[800,128]{1,0:T(8,128)(2,1)S(1)} %unit.1), channel_id=1, source_target_pairs={{0,2},{1,3},{2,0},{3,1},{4,6},{5,7},{6,4},{7,5},{8,10},{9,11},{10,... | collective-permute-start | bytes 614408 | tf_op jit(solution)/shard_map/ppermute | solution.py:51
  5.9 6.2 %collective-permute-start.2 = (bf16[800,128]{1,0:T(8,128)(2,1)S(1)}, bf16[800,128]{1,0:T(8,128)(2,1)S(1)}, u32[]{:S(2)}, u32[]{:S(2)}) collective-permute-start(bf16[800,128]{1,0:T(8,128)(2,1)S(1)} %unit.1), channel_id=1, source_target_pairs={{0,3},{1,0},{2,1},{3,2},{4,7},{5,4},{6,5},{7,6},{8,11},{9,8},{10,9... | collective-permute-start | bytes 614408 | tf_op jit(solution)/shard_map/ppermute | solution.py:51
  6.7 6.1 %collective-permute-start.1 = (bf16[800,128]{1,0:T(8,128)(2,1)S(1)}, bf16[800,128]{1,0:T(8,128)(2,1)S(1)}, u32[]{:S(2)}, u32[]{:S(2)}) collective-permute-start(bf16[800,128]{1,0:T(8,128)(2,1)S(1)} %unit.1), channel_id=1, source_target_pairs={{0,1},{1,2},{2,3},{3,0},{4,5},{5,6},{6,7},{7,4},{8,9},{9,10},{10,1... | collective-permute-start | bytes 614408 | tf_op jit(solution)/shard_map/ppermute | solution.py:51
  13.3 10.3 %collective-permute-start.5 = (bf16[1600,128]{1,0:T(8,128)(2,1)S(1)}, bf16[1600,128]{1,0:T(8,128)(2,1)S(1)}, u32[]{:S(2)}, u32[]{:S(2)}) collective-permute-start(bf16[1600,128]{1,0:T(8,128)(2,1)S(1)} %constant_dynamic-update-slice_fusion.2.refs_1_), channel_id=1, source_target_pairs={{0,12},{1,13},{2,14},{3,15},{4,0},{5,1},{6,2},{7,3},{8,4},{9,5},{1... | collective-permute-start | bytes 1228808 | tf_op jit(solution)/shard_map/ppermute | solution.py:56
  15.6 8.4 %collective-permute-start.4 = (bf16[1600,128]{1,0:T(8,128)(2,1)S(1)}, bf16[1600,128]{1,0:T(8,128)(2,1)S(1)}, u32[]{:S(2)}, u32[]{:S(2)}) collective-permute-start(bf16[1600,128]{1,0:T(8,128)(2,1)S(1)} %constant_dynamic-update-slice_fusion.refs_0_), channel_id=1, source_target_pairs={{0,4},{1,5},{2,6},{3,7},{4,8},{5,9},{6,10},{7,11},{8,12},{9,13},{1... | collective-permute-start | bytes 1228808 | tf_op jit(solution)/shard_map/ppermute | solution.py:56
  16.6 11.7 %collective-permute-start.6 = (bf16[1600,128]{1,0:T(8,128)(2,1)S(1)}, bf16[1600,128]{1,0:T(8,128)(2,1)S(1)}, u32[]{:S(2)}, u32[]{:S(2)}) collective-permute-start(bf16[1600,128]{1,0:T(8,128)(2,1)S(1)} %constant_dynamic-update-slice_fusion.2.refs_1_), channel_id=1, source_target_pairs={{0,4},{1,5},{2,6},{3,7},{4,8},{5,9},{6,10},{7,11},{8,12},{9,13},{1... | collective-permute-start | bytes 1228808 | tf_op jit(solution)/shard_map/ppermute | solution.py:56
  16.8 11.5 %collective-permute-start.7 = (bf16[1600,128]{1,0:T(8,128)(2,1)S(1)}, bf16[1600,128]{1,0:T(8,128)(2,1)S(1)}, u32[]{:S(2)}, u32[]{:S(2)}) collective-permute-start(bf16[1600,128]{1,0:T(8,128)(2,1)S(1)} %constant_dynamic-update-slice_fusion.refs_0_), channel_id=1, source_target_pairs={{0,12},{1,13},{2,14},{3,15},{4,0},{5,1},{6,2},{7,3},{8,4},{9,5},{1... | collective-permute-start | bytes 1228808 | tf_op jit(solution)/shard_map/ppermute | solution.py:56
  23.9 10.1 %collective-permute-start.8 = (bf16[1600,128]{1,0:T(8,128)(2,1)S(1)}, bf16[1600,128]{1,0:T(8,128)(2,1)S(1)}, u32[]{:S(2)}, u32[]{:S(2)}) collective-permute-start(bf16[1600,128]{1,0:T(8,128)(2,1)S(1)} %collective-permute-done.4.refs_0_.refs_2_), channel_id=1, source_target_pairs={{0,4},{1,5},{2,6},{3,7},{4,8},{5,9},{6,10},{7,11},{8,12},{9,13},{1... | collective-permute-start | bytes 1228808 | tf_op jit(solution)/shard_map/ppermute | solution.py:56
  23.9 10.1 %collective-permute-start.9 = (bf16[1600,128]{1,0:T(8,128)(2,1)S(1)}, bf16[1600,128]{1,0:T(8,128)(2,1)S(1)}, u32[]{:S(2)}, u32[]{:S(2)}) collective-permute-start(bf16[1600,128]{1,0:T(8,128)(2,1)S(1)} %collective-permute-done.5.refs_3_.refs_5_), channel_id=1, source_target_pairs={{0,12},{1,13},{2,14},{3,15},{4,0},{5,1},{6,2},{7,3},{8,4},{9,5},{1... | collective-permute-start | bytes 1228808 | tf_op jit(solution)/shard_map/ppermute | solution.py:56
  36.9 4.6 %collective-permute-start.10 = (bf16[3,800,128]{2,1,0:T(8,128)(2,1)S(1)}, bf16[3,800,128]{2,1,0:T(8,128)(2,1)S(1)}, u32[]{:S(2)}, u32[]{:S(2)}) collective-permute-start(bf16[3,800,128]{2,1,0:T(8,128)(2,1)S(1)} %get-tuple-element.70), channel_id=1, source_target_pairs={{0,16},{1,17},{2,18},{3,19},{4,20},{5,21},{6,22},{7,23},{8,24},{9,... | collective-permute-start | bytes 1843208 | tf_op jit(solution)/shard_map/ppermute | solution.py:46
  41.7 17.6 %copy-start = (bf16[1,32,3,256]{3,1,2,0:T(8,128)(2,1)S(1)}, bf16[1,32,3,256]{3,1,2,0:T(8,128)(2,1)}, u32[]{:S(2)}) copy-start(bf16[1,32,3,256]{3,1,2,0:T(8,128)(2,1)} %param.10) | copy-start | bytes 147460
  41.7 17.6 %collective-permute-start.11 = (bf16[800,128]{1,0:T(8,128)(2,1)S(1)}, bf16[800,128]{1,0:T(8,128)(2,1)S(1)}, u32[]{:S(2)}, u32[]{:S(2)}) collective-permute-start(bf16[800,128]{1,0:T(8,128)(2,1)S(1)} %get-tuple-element.74), channel_id=1, source_target_pairs={{0,32},{1,33},{2,34},{3,35},{4,36},{5,37},{6,38},{7,39},{8,40},{9,... | collective-permute-start | bytes 614408 | tf_op jit(solution)/shard_map/ppermute | solution.py:60
  44.6 14.6 %collective-permute-start.12 = (bf16[800,128]{1,0:T(8,128)(2,1)S(1)}, bf16[800,128]{1,0:T(8,128)(2,1)S(1)}, u32[]{:S(2)}, u32[]{:S(2)}) collective-permute-start(bf16[800,128]{1,0:T(8,128)(2,1)S(1)} %get-tuple-element.75), channel_id=1, source_target_pairs={{0,96},{1,97},{2,98},{3,99},{4,100},{5,101},{6,102},{7,103},{8,104... | collective-permute-start | bytes 614408 | tf_op jit(solution)/shard_map/ppermute | solution.py:60
  48.0 11.3 %collective-permute-start.13 = (bf16[800,128]{1,0:T(8,128)(2,1)S(1)}, bf16[800,128]{1,0:T(8,128)(2,1)S(1)}, u32[]{:S(2)}, u32[]{:S(2)}) collective-permute-start(bf16[800,128]{1,0:T(8,128)(2,1)S(1)} %get-tuple-element.76), channel_id=1, source_target_pairs={{0,64},{1,65},{2,66},{3,67},{4,68},{5,69},{6,70},{7,71},{8,72},{9,... | collective-permute-start | bytes 614408 | tf_op jit(solution)/shard_map/ppermute | solution.py:60
where the time goes:
time: 60.2 us; the launch traced here: 60.3 us
  Pallas kernels  27.5 us (46%)
  starting transfers between devices  24 us (40%)
  blocking collectives  4.58 us (8%)
  waiting for transfers between devices  2.94 us (5%)
  other arithmetic  0.66 us (1%)
    pallas_call x5, Pallas kernels, near(): pl.pallas_call(functools.partial(near_kernel, first_unit, count, part), o...  19.8 us
    ppermute x6, starting transfers between devices, along_second(): return lax.ppermute(value, AXES, routes(move))  7.8 us
    ppermute x3, starting transfers between devices, along_z(): lax.ppermute(value, AXES, routes(lambda z, c, y, x: (z + step, c, y, x)))  7.55 us
    pallas_call x1, Pallas kernels, make_points(): pl.pallas_call(points_kernel, out_shape=(jax.ShapeDtypeStruct((32, 4, HAL...  4.6 us
    all_to_all x1, blocking collectives, local(): lax.all_to_all(pair, 'row', 0, 0, axis_index_groups=chips, tiled=True)  4.58 us
    ppermute x3, starting transfers between devices, along_first(): return lax.ppermute(value, AXES, routes(move))  4.54 us
    ppermute x2, starting transfers between devices, swap_core(): lax.ppermute(value, AXES, routes(lambda z, c, y, x: (z, 1 - c, y, x)))  4.13 us
    ppermute x6, waiting for transfers between devices, along_second(): return lax.ppermute(value, AXES, routes(move))  2.05 us
  transfers between devices with their start and end apart: 14, of which 4 were waited for; matrix products, arithmetic and copies ran while one was open for 1% of the time, Pallas kernels for 39%

commit v1 on v0

--- a/solution.py
+++ b/solution.py
@@ -18,7 +18,8 @@
 AXES = ("row", "col")
 TARGETS = ((1, 0), (2, 0), (3, 0), (1, 1), (2, 1), (3, 1), (0, 0), (0, 1))
 AWAY = 6
-SPANS = {"first": (0, AWAY), "middle": (0, AWAY), "send": (3, AWAY), "keep": (0, 3), "own": (AWAY, 8)}
+LINE, OUTER, INNER = 0, 5, 2
+SPANS = {"first": (0, 8), "middle": (0, AWAY), "send": (3, AWAY), "keep": (0, 3), "own": (AWAY, 8)}
 SIDE = 4
 
 eps_square = 0.0004
@@ -47,17 +48,17 @@
 
 
 def along_first(value, step):
-    move = lambda z, c, y, x: (z, c, y, x + step) if c == 0 else (z, c, y + step, x)
+    move = lambda z, c, y, x: (z, c, y + step, x) if c == 0 else (z + step, c, y, x)
     return lax.ppermute(value, AXES, routes(move))
 
 
 def along_second(value, step):
-    move = lambda z, c, y, x: (z, c, y + step, x) if c == 0 else (z, c, y, x + step)
+    move = lambda z, c, y, x: (z + step, c, y, x) if c == 0 else (z, c, y + step, x)
     return lax.ppermute(value, AXES, routes(move))
 
 
-def along_z(value, step):
-    return lax.ppermute(value, AXES, routes(lambda z, c, y, x: (z + step, c, y, x)))
+def along_line(value, step):
+    return lax.ppermute(value, AXES, routes(lambda z, c, y, x: (z, c, y, x + step)))
 
 
 def whole(count):
@@ -154,7 +155,7 @@
     for copy in first:
         copy.wait()
     for t, (step, other) in enumerate(TARGETS):
-        cluster = ((step + z) & 3) * 32 + ((other + core) & 1) * 16 + y * SIDE + x
+        cluster = (((step + z) & 3) << LINE) + ((other + core) & 1) * 16 + (y << OUTER) + (x << INNER)
         for i in range(3):
             targets_ref[t, i : i + 1, :] = positions[i, pl.ds(cluster, 1), :]
         targets_ref[t, 3:4, :] = areas[pl.ds(cluster, 1), :]
@@ -162,7 +163,7 @@
         first, second = back[(s >> 1) & 3], back[s >> 3]
         on_x = (x + jnp.where(core == 0, first, second)) & 3
         on_y = (y + jnp.where(core == 0, second, first)) & 3
-        cluster = z * 32 + ((s + core) & 1) * 16 + on_y * SIDE + on_x
+        cluster = (z << LINE) + ((s + core) & 1) * 16 + (on_y << OUTER) + (on_x << INNER)
         for i in range(3):
             columns[s, i : i + 1, :] = half(positions[i, pl.ds(cluster, 1), :])
         columns[s, 3:4, :] = half(areas[pl.ds(cluster, 1), :])
@@ -235,7 +236,7 @@
     elif part == "keep":
         carried, far, refs = refs[0], refs[1], refs[2:]
     elif part == "own":
-        far, refs = refs[0], refs[1:]
+        carried, far, refs = refs[0], refs[1], refs[2:]
     if part == "send":
         send, far, acc, refs = refs[0], refs[1], refs[2], refs[3:]
     elif sums_far:
@@ -260,7 +261,7 @@
     for k in range(6):
         entry[entries + k] = low * 64 + 2 * first_unit
     near_rows = slice(0, 3 * CS)
-    if part in ("first", "own"):
+    if part == "first":
         acc[:, near_rows] = jnp.zeros((high - low, 3 * CS, LOADS), f32)
     else:
         acc[:, near_rows] = carried[low:high]
@@ -273,7 +274,9 @@
             for k in range(4):
                 at = u * 128 + k * RANK
                 wide[at : at + RANK, k * LOADS : (k + 1) * LOADS] = moments
-        coefficients = dot32(blocks[...], wide[...])
+        coefficients = dot32(
+            blocks[:, first_unit * 128 : (first_unit + units) * 128], wide[...]
+        )
         for k in range(4):
             piece = coefficients[:, k * LOADS : (k + 1) * LOADS]
             far[k] = piece if part == "first" else carried_far[k] + piece
@@ -359,7 +362,7 @@
 def near(part, first_unit, buffers, carried, counts, targets, spread, blocks):
     count = len(buffers)
     slots = 4 * count
-    sums = jax.ShapeDtypeStruct((AWAY, 3 * CS, LOADS), f32)
+    sums = jax.ShapeDtypeStruct((SPANS[part][1], 3 * CS, LOADS), f32)
     far = jax.ShapeDtypeStruct((4, 64, LOADS), f32)
     scratch = [
         pltpu.VMEM((count * 2 * UNIT, LOADS), bf16),
@@ -374,7 +377,7 @@
         if part == "own":
             shapes += (jax.ShapeDtypeStruct((2, FULL, LOADS), bf16),)
     else:
-        operands.append(blocks[:, first_unit * 128 : (first_unit + 2 * count) * 128])
+        operands.append(blocks)
         scratch.append(pltpu.VMEM((2 * count * 128, 4 * LOADS), bf16))
         shapes = (sums, far)
         if part == "send":
@@ -437,13 +440,13 @@
 def local(densities, positions, areas, bases, near_pairs, far_pairs, couplings):
     row = lax.axis_index("row")
     col = lax.axis_index("col")
-    z, core = row >> 1, row & 1
-    y, x = col >> 2, col & 3
+    core, here = row & 1, (row >> 1) * 32 + col
+    z, y, x = ((here >> shift) & 3 for shift in (LINE, OUTER, INNER))
     first_at = jnp.where(core == 0, x, y)
     second_at = jnp.where(core == 0, y, x)
 
     def unit_of(cluster):
-        on_y, on_x = (cluster >> 2) & 3, cluster & 3
+        on_y, on_x = (cluster >> OUTER) & 3, (cluster >> INNER) & 3
         first = (jnp.where(core == 0, on_x, on_y) - first_at) & 3
         second = (jnp.where(core == 0, on_y, on_x) - second_at) & 3
         put = lambda r: jnp.where(r == 0, 0, jnp.where(r == 1, 2, jnp.where(r == 2, 3, 1)))
@@ -453,12 +456,13 @@
         return ((cluster >> 4) + core) & 1
 
     def slot_of(cluster):
-        return jnp.where(cluster >> 5 == z, unit_of(cluster) * 2 + other_core(cluster), -1)
+        return jnp.where(((cluster >> LINE) & 3) == z, unit_of(cluster) * 2 + other_core(cluster), -1)
 
     def target_of(cluster):
-        step, other = ((cluster >> 5) - z) & 3, other_core(cluster)
+        step, other = ((cluster >> LINE) - z) & 3, other_core(cluster)
         place = jnp.where(step == 0, AWAY + other, other * 3 + step - 1)
-        return jnp.where((cluster & 15) == col, place, -1)
+        same = (((cluster >> OUTER) & 3) == y) & (((cluster >> INNER) & 3) == x)
+        return jnp.where(same, place, -1)
 
     bases = jnp.transpose(bases, (0, 2, 1, 3))
     positions = jnp.transpose(positions, (1, 0, 2))
@@ -466,22 +470,13 @@
     partner = swap_core(densities)
     own, moments, flip = moments_of(core, densities, bases)
     unit = make_unit(core, own, partner, moments)
+    from_across = along_first(unit, 2)
+    from_above = along_first(unit, -1)
     from_below = along_first(unit, 1)
-    from_above = along_first(unit, -1)
-    from_across = along_first(unit, 2)
     here = jnp.stack([z, core, y, x]).astype(jnp.int32)
     here, unit = lax.optimization_barrier((here, unit))
     spread, targets, couplings = make_points(here, positions, areas, couplings)
-    (near_pairs, far_pairs, couplings, spread, targets, unit, from_below, from_above, from_across) = (
-        lax.optimization_barrier(
-            (near_pairs, far_pairs, couplings, spread, targets, unit)
-            + (from_below, from_above, from_across)
-        )
-    )
-    low = jnp.concatenate([unit, from_below], axis=0)
-    high = jnp.concatenate([from_above, from_across], axis=0)
-    low_below = along_second(low, 1)
-    high_above = along_second(high, -1)
+    near_pairs, far_pairs, spread = lax.optimization_barrier((near_pairs, far_pairs, spread))
 
     heads, tails = near_pairs[:, 0], near_pairs[:, 1]
     mark = lambda index, size: index[None, :] == jnp.arange(size, dtype=jnp.int32)[:, None]
@@ -505,12 +500,22 @@
 
     back_cell = jnp.where(far_heads != far_tails, cell(far_tails, far_heads), -1)
     blocks = make_blocks(cell(far_heads, far_tails), back_cell, couplings, flip)
-    blocks, low_later, high_later = lax.optimization_barrier((blocks, low, high))
-    high_below = along_second(high_later, 1)
-    low_above = along_second(low_later, -1)
+    (spread, targets, counts, blocks, unit, from_below, from_above, from_across) = (
+        lax.optimization_barrier(
+            (spread, targets, counts, blocks, unit, from_below, from_above, from_across)
+        )
+    )
+    low = jnp.concatenate([unit, from_below], axis=0)
+    high = jnp.concatenate([from_above, from_across], axis=0)
+    low_below = along_second(low, 1)
+    high_above = along_second(high, -1)
+
+    high_below = along_second(high, 1)
+    low_above = along_second(low, -1)
     tables = (counts, targets, spread)
 
     carried = near("first", 0, (low, high), (), *tables, blocks)
+    started = carried[0]
     low_below, high_above, carried = lax.optimization_barrier((low_below, high_above, carried))
     low_across = along_second(low_below, 1)
     high_across = along_second(high_above, -1)
@@ -522,10 +527,9 @@
     (keep,) = near("keep", 12, across, (carried[0], far), *tables, blocks)
     both = [(keep[k] + swapped[k].astype(f32)).astype(bf16) for k in range(3)]
     both, far = lax.optimization_barrier((both, far))
-    others = [along_z(both[0], 1), along_z(both[2], 3)]
-    others.append(along_z(both[1], 2))
-    everything = (low, high) + beside + across
-    own, pair = near("own", 0, everything, (far,), *tables, blocks)
+    two_hops = along_line(both[1], 2)
+    others = [two_hops, along_line(both[0], 1), along_line(both[2], 3)]
+    own, pair = near("own", 4, beside + across, (started, far), *tables, blocks)
     chips = [[2 * k, 2 * k + 1] for k in range(SIDE)]
     swapped = lax.all_to_all(pair, "row", 0, 0, axis_index_groups=chips, tiled=True)
     return finish(core, own, swapped, others, bases)

time: 60.2 us -> 59.9 us (level)
  Pallas kernels: 27.5 us -> 28.8 us
  blocking collectives: 4.58 us -> 3.67 us
    pallas_call x5, Pallas kernels: 19.8 us -> 21.1 us  [near(): pl.pallas_call(functools.partial(near_kernel, first_unit, count, part), o...]
    ppermute x2, starting transfers between devices: 4.13 us -> 2.94 us  [swap_core(): lax.ppermute(value, AXES, routes(lambda z, c, y, x: (z, 1 - c, y, x)))]
    all_to_all x1, blocking collectives: 4.58 us -> 3.67 us  [local(): lax.all_to_all(pair, 'row', 0, 0, axis_index_groups=chips, tiled=True)]
    ppermute x3, waiting for transfers between devices: 0.72 us -> 0.02 us  [along_first(): return lax.ppermute(value, AXES, routes(move))]
    ppermute x3, starting transfers between devices: 4.54 us -> 5.23 us  [along_first(): return lax.ppermute(value, AXES, routes(move))]
  transfers between devices with their start and end apart: 14 -> 14, of which waited for: 4 -> 5; matrix products, arithmetic and copies ran while one was open for 1% -> 1% of each run, Pallas kernels for 39% -> 41%
where the time goes in v1:
time: 59.9 us; the launch traced here: 59.8 us
  Pallas kernels  28.8 us (48%)
  starting transfers between devices  23.5 us (39%)
  blocking collectives  3.67 us (6%)
  waiting for transfers between devices  2.57 us (4%)
  other arithmetic  0.68 us (1%)
    pallas_call x5, Pallas kernels, near(): pl.pallas_call(functools.partial(near_kernel, first_unit, count, part), o...  21.1 us
    ppermute x6, starting transfers between devices, along_second(): return lax.ppermute(value, AXES, routes(move))  8.29 us
    ppermute x3, starting transfers between devices, along_line(): lax.ppermute(value, AXES, routes(lambda z, c, y, x: (z, c, y, x + step)))  7.02 us
    ppermute x3, starting transfers between devices, along_first(): return lax.ppermute(value, AXES, routes(move))  5.23 us
    pallas_call x1, Pallas kernels, make_points(): pl.pallas_call(points_kernel, out_shape=(jax.ShapeDtypeStruct((32, 4, HAL...  4.6 us
    all_to_all x1, blocking collectives, local(): lax.all_to_all(pair, 'row', 0, 0, axis_index_groups=chips, tiled=True)  3.67 us
    ppermute x2, starting transfers between devices, swap_core(): lax.ppermute(value, AXES, routes(lambda z, c, y, x: (z, 1 - c, y, x)))  2.94 us
    ppermute x6, waiting for transfers between devices, along_second(): return lax.ppermute(value, AXES, routes(move))  1.97 us
  transfers between devices with their start and end apart: 14, of which 5 were waited for; matrix products, arithmetic and copies ran while one was open for 1% of the time, Pallas kernels for 41%

profile of v1, /device:TPU:1, one launch (start us, length us, event | category | flops | bytes accessed | tf_op | source)
XLA Modules:
  0.0 59.8 jit_solution(10639714464066965943)
XLA Ops:
  0.0 1.4 %collective-permute-start = (bf16[1,3,256,128]{3,2,1,0:T(8,128)(2,1)}, bf16[1,3,256,128]{3,2,1,0:T(8,128)(2,1)S(1)}, u32[]{:S(2)}, u32[]{:S(2)}) collective-permute-start(bf16[1,3,256,128]{3,2,1,0:T(8,128)(2,1)} %dens_ref.1), channel_id=1, source_target_pairs={{0,16},{1,17},{2,18},{3,19},{4,20},{5,21},{6,22},{7,23},{8,24},{9,... | collective-permute-start | bytes 589832 | tf_op jit(solution)/shard_map/ppermute | solution.py:47
  1.4 1.1 %moments.1 = (bf16[384,128]{1,0:T(8,128)(2,1)S(1)}, bf16[32,128]{1,0:T(8,128)(2,1)S(1)}, bf16[1024,1024]{1,0:T(8,128)(2,1)S(1)}) custom-call(s32[1]{0:T(128)} %bitcast.core_ref.core, bf16[1,3,256,128]{3,2,1,0:T(8,128)(2,1)} %dens_ref.1, bf16[1,3,32,256]{3,2,1,0:T(8,128)(2,1)} %bitcast.68), custom_call_target="tpu_custom_call" | custom-call | tf_op jit(solution)/shard_map/moments/pallas_call | solution.py:106
  2.6 0.1 pad_add_fusion.2.here_ref
  2.6 0.1 collective-permute-done.partner_ref
  2.7 0.1 unit.1
  2.8 3.8 %collective-permute-start.3 = (bf16[800,128]{1,0:T(8,128)(2,1)S(1)}, bf16[800,128]{1,0:T(8,128)(2,1)S(1)}, u32[]{:S(2)}, u32[]{:S(2)}) collective-permute-start(bf16[800,128]{1,0:T(8,128)(2,1)S(1)} %unit.1), channel_id=1, source_target_pairs={{0,8},{1,9},{2,10},{3,11},{4,12},{5,13},{6,14},{7,15},{8,0},{9,1},... | collective-permute-start | bytes 614408 | tf_op jit(solution)/shard_map/ppermute | solution.py:52
  6.6 0.4 collective-permute-start.2
  7.0 1.0 %collective-permute-start.1 = (bf16[800,128]{1,0:T(8,128)(2,1)S(1)}, bf16[800,128]{1,0:T(8,128)(2,1)S(1)}, u32[]{:S(2)}, u32[]{:S(2)}) collective-permute-start(bf16[800,128]{1,0:T(8,128)(2,1)S(1)} %unit.1), channel_id=1, source_target_pairs={{0,4},{1,5},{2,6},{3,7},{4,8},{5,9},{6,10},{7,11},{8,12},{9,13},{1... | collective-permute-start | bytes 614408 | tf_op jit(solution)/shard_map/ppermute | solution.py:52
  8.0 4.6 %points.1 = (f32[32,4,128,128]{3,2,1,0:T(8,128)S(1)}, f32[8,8,256]{2,1,0:T(8,128)S(1)}, bf16[768,1024]{1,0:T(8,128)(2,1)S(1)}) custom-call(s32[4]{0:T(128)S(1)} %pad_add_fusion.2.here_ref, f32[3,128,256]{2,1,0:T(8,128)} %bitcast.70, f32[128,256]{1,0:T(8,128)} %areas_ref.1, bf16[768,1024]{1,0:T(8,128)(2,1)} %couplings_ref.1), custom_call_target="tpu_custom_call" | custom-call | tf_op jit(solution)/shard_map/points/pallas_call | solution.py:178
  12.6 0.0 copy-done.1
  12.6 0.1 and_reduce_fusion.1
  12.7 0.2 fusion.27
  13.0 0.0 copy-done.2
  13.0 0.1 bitcast_select_fusion.1
  13.1 0.9 %coupling_blocks.1.refs_2_.refs_4_ = bf16[64,2048]{1,0:T(8,128)(2,1)S(1)} custom-call(s32[1,768]{1,0:T(1,128)S(1)} %get-tuple-element.86.forward_ref, s32[1,768]{1,0:T(1,128)S(1)} %get-tuple-element.85.backward_ref, bf16[768,1024]{1,0:T(8,128)(2,1)S(1)} %get-tuple-element.48.couplings_ref, bf16[1024,1024]{1,0:T(8,128)(2,1)S(1)} %get-tuple-element.49.flip_ref), custom_call_target="tpu_custom_call" | custom-call | tf_op jit(solution)/shard_map/coupling_blocks/pallas_call | solution.py:216
  14.1 0.2 fusion.2.counts
  14.3 0.0 collective-permute-done.3
  14.3 0.0 collective-permute-done.2
  14.3 0.0 collective-permute-done.1
  14.4 2.8 %collective-permute-start.5 = (bf16[1600,128]{1,0:T(8,128)(2,1)S(1)}, bf16[1600,128]{1,0:T(8,128)(2,1)S(1)}, u32[]{:S(2)}, u32[]{:S(2)}) collective-permute-start(bf16[1600,128]{1,0:T(8,128)(2,1)S(1)} %constant_dynamic-update-slice_fusion.2.refs_1_), channel_id=1, source_target_pairs={{0,96},{1,97},{2,98},{3,99},{4,100},{5,101},{6,102},{7,103},{8,104... | collective-permute-start | bytes 1228808 | tf_op jit(solution)/shard_map/ppermute | solution.py:57
  17.2 0.1 collective-permute-start.4
  17.3 0.1 collective-permute-start.6
  17.4 2.7 %collective-permute-start.7 = (bf16[1600,128]{1,0:T(8,128)(2,1)S(1)}, bf16[1600,128]{1,0:T(8,128)(2,1)S(1)}, u32[]{:S(2)}, u32[]{:S(2)}) collective-permute-start(bf16[1600,128]{1,0:T(8,128)(2,1)S(1)} %constant_dynamic-update-slice_fusion.refs_0_), channel_id=1, source_target_pairs={{0,96},{1,97},{2,98},{3,99},{4,100},{5,101},{6,102},{7,103},{8,104... | collective-permute-start | bytes 1228808 | tf_op jit(solution)/shard_map/ppermute | solution.py:57
  20.0 5.3 %near_first.1 = (f32[8,768,128]{2,1,0:T(8,128)S(1)}, f32[4,64,128]{2,1,0:T(8,128)S(1)}) custom-call(s32[8,32]{1,0:T(8,128)S(1)} %fusion.2.counts, f32[8,8,256]{2,1,0:T(8,128)S(1)} %get-tuple-element.52.targets, f32[32,4,128,128]{3,2,1,0:T(8,128)S(1)} %get-tuple-element.53.spread, bf16[1600,128]{1,0:T(8,128)(2,1)S(1)} %constant_dynamic-update-slice_fusion.refs_0_, ...), custom_call_target="tpu_custom_call" | custom-call | flops 2000000000 | bytes 8000000 | tf_op jit(solution)/shard_map/near_first/pallas_call | solution.py:387
  25.3 0.0 collective-permute-done.5.refs_3_
  25.3 0.2 collective-permute-done.4.refs_0_
  25.6 0.0 collective-permute-start.8
  25.6 2.7 %collective-permute-start.9 = (bf16[1600,128]{1,0:T(8,128)(2,1)S(1)}, bf16[1600,128]{1,0:T(8,128)(2,1)S(1)}, u32[]{:S(2)}, u32[]{:S(2)}) collective-permute-start(bf16[1600,128]{1,0:T(8,128)(2,1)S(1)} %collective-permute-done.5.refs_3_), channel_id=1, source_target_pairs={{0,96},{1,97},{2,98},{3,99},{4,100},{5,101},{6,102},{7,103},{8,104... | collective-permute-start | bytes 1228808 | tf_op jit(solution)/shard_map/ppermute | solution.py:57
  28.3 1.7 %collective-permute-done.6.refs_1_ = bf16[1600,128]{1,0:T(8,128)(2,1)S(1)} collective-permute-done((bf16[1600,128]{1,0:T(8,128)(2,1)S(1)}, bf16[1600,128]{1,0:T(8,128)(2,1)S(1)}, u32[]{:S(2)}, u32[]{:S(2)}) %collective-permute-start.6) | collective-permute-done | bytes 409632 | tf_op jit(solution)/shard_map/ppermute | solution.py:57
  30.0 0.0 collective-permute-done.7.refs_2_
  30.0 7.8 %near_middle.1 = (f32[6,768,128]{2,1,0:T(8,128)S(1)}, f32[4,64,128]{2,1,0:T(8,128)S(1)}) custom-call(s32[8,32]{1,0:T(8,128)S(1)} %fusion.2.counts, f32[8,8,256]{2,1,0:T(8,128)S(1)} %get-tuple-element.52.targets, f32[32,4,128,128]{3,2,1,0:T(8,128)S(1)} %get-tuple-element.53.spread, bf16[1600,128]{1,0:T(8,128)(2,1)S(1)} %collective-permute-done.4.refs_0_, ...), custom_call_target="tpu_custom_call" | custom-call | flops 4000000000 | bytes 8000000 | tf_op jit(solution)/shard_map/near_middle/pallas_call | solution.py:387
  37.8 0.0 collective-permute-done.8.refs_0_.refs_4_
  37.8 0.0 collective-permute-done.9.refs_1_.refs_5_
  37.8 3.2 %near_send.1 = (bf16[3,800,128]{2,1,0:T(8,128)(2,1)S(1)}, f32[4,64,128]{2,1,0:T(8,128)S(1)}) custom-call(s32[8,32]{1,0:T(8,128)S(1)} %fusion.2.counts, f32[8,8,256]{2,1,0:T(8,128)S(1)} %get-tuple-element.52.targets, f32[32,4,128,128]{3,2,1,0:T(8,128)S(1)} %get-tuple-element.53.spread, bf16[1600,128]{1,0:T(8,128)(2,1)S(1)} %collective-permute-done.8.refs_0_.refs_4_, ...), custom_call_target="tpu_custom_call" | custom-call | flops 2000000000 | bytes 8000000 | tf_op jit(solution)/shard_map/near_send/pallas_call | solution.py:387
  41.0 1.5 %collective-permute-start.10 = (bf16[3,800,128]{2,1,0:T(8,128)(2,1)S(1)}, bf16[3,800,128]{2,1,0:T(8,128)(2,1)S(1)}, u32[]{:S(2)}, u32[]{:S(2)}) collective-permute-start(bf16[3,800,128]{2,1,0:T(8,128)(2,1)S(1)} %get-tuple-element.68), channel_id=1, source_target_pairs={{0,16},{1,17},{2,18},{3,19},{4,20},{5,21},{6,22},{7,23},{8,24},{9,... | collective-permute-start | bytes 1843208 | tf_op jit(solution)/shard_map/ppermute | solution.py:47
  42.5 1.5 %near_keep.1 = f32[3,800,128]{2,1,0:T(8,128)S(1)} custom-call(s32[8,32]{1,0:T(8,128)S(1)} %fusion.2.counts, f32[8,8,256]{2,1,0:T(8,128)S(1)} %get-tuple-element.52.targets, f32[32,4,128,128]{3,2,1,0:T(8,128)S(1)} %get-tuple-element.53.spread, bf16[1600,128]{1,0:T(8,128)(2,1)S(1)} %collective-permute-done.8.refs_0_.refs_4_, ...), custom_call_target="tpu_custom_call" | custom-call | flops 2000000000 | bytes 8000000 | tf_op jit(solution)/shard_map/near_keep/pallas_call | solution.py:387
  44.1 0.1 collective-permute-done.10
  44.2 0.1 fusion.9
  44.4 0.0 copy-start
  44.4 4.3 %collective-permute-start.11 = (bf16[800,128]{1,0:T(8,128)(2,1)S(1)}, bf16[800,128]{1,0:T(8,128)(2,1)S(1)}, u32[]{:S(2)}, u32[]{:S(2)}) collective-permute-start(bf16[800,128]{1,0:T(8,128)(2,1)S(1)} %get-tuple-element.72), channel_id=1, source_target_pairs={{0,2},{1,3},{2,0},{3,1},{4,6},{5,7},{6,4},{7,5},{8,10},{9,11},{10,... | collective-permute-start | bytes 614408 | tf_op jit(solution)/shard_map/ppermute | solution.py:61
  48.7 0.2 collective-permute-start.12
  48.9 2.5 %collective-permute-start.13 = (bf16[800,128]{1,0:T(8,128)(2,1)S(1)}, bf16[800,128]{1,0:T(8,128)(2,1)S(1)}, u32[]{:S(2)}, u32[]{:S(2)}) collective-permute-start(bf16[800,128]{1,0:T(8,128)(2,1)S(1)} %get-tuple-element.74), channel_id=1, source_target_pairs={{0,3},{1,0},{2,1},{3,2},{4,7},{5,4},{6,5},{7,6},{8,11},{9,8},{10,9... | collective-permute-start | bytes 614408 | tf_op jit(solution)/shard_map/ppermute | solution.py:61
  51.4 3.3 %near_own.1 = (f32[2,800,128]{2,1,0:T(8,128)S(1)}, bf16[2,800,128]{2,1,0:T(8,128)(2,1)S(1)}) custom-call(s32[8,32]{1,0:T(8,128)S(1)} %fusion.2.counts, f32[8,8,256]{2,1,0:T(8,128)S(1)} %get-tuple-element.52.targets, f32[32,4,128,128]{3,2,1,0:T(8,128)S(1)} %get-tuple-element.53.spread, bf16[1600,128]{1,0:T(8,128)(2,1)S(1)} %collective-permute-done.4.refs_0_, ...), custom_call_target="tpu_custom_call" | custom-call | flops 6000000000 | bytes 8000000 | tf_op jit(solution)/shard_map/near_own/pallas_call | solution.py:387
  54.7 3.7 %all_to_all.5.swapped = bf16[2,800,128]{2,1,0:T(8,128)(2,1)S(1)} all-to-all(bf16[2,800,128]{2,1,0:T(8,128)(2,1)S(1)} %get-tuple-element.71), channel_id=1, replica_groups={{0,16},{32,48},{64,80},{96,112},{1,17},{33,49},{65,81},{97,113},{2,18},..., dimensions={0} | all-to-all | bytes 819200 | tf_op jit(solution)/shard_map/all_to_all | solution.py:534
  58.4 0.0 collective-permute-done.11.one
  58.4 0.4 collective-permute-done.12.two
  58.7 0.0 collective-permute-done.13.three
  58.7 1.0 %sum_and_expand.1 = bf16[1,3,256,128]{3,2,1,0:T(8,128)(2,1)} custom-call(s32[1]{0:T(128)} %bitcast.core_ref.core, f32[2,800,128]{2,1,0:T(8,128)S(1)} %get-tuple-element.70.keep, bf16[2,800,128]{2,1,0:T(8,128)(2,1)S(1)} %all_to_all.5.swapped, bf16[800,128]{1,0:T(8,128)(2,1)S(1)} %collective-permute-done.11.one, ...), custom_call_target="tpu_custom_call" | custom-call | tf_op jit(solution)/shard_map/sum_and_expand/pallas_call | solution.py:430
  (11 shorter events, 0.1 us)
Async XLA Ops:
  0.0 13.0 %copy-start.2 = (s32[768,2]{0,1:T(2,128)S(1)}, s32[768,2]{0,1:T(2,128)}, u32[]{:S(2)}) copy-start(s32[768,2]{0,1:T(2,128)} %param.12) | copy-start | bytes 18436
  0.0 12.6 %copy-start.1 = (s32[1920,2]{0,1:T(2,128)S(1)}, s32[1920,2]{0,1:T(2,128)}, u32[]{:S(2)}) copy-start(s32[1920,2]{0,1:T(2,128)} %param.11) | copy-start | bytes 46084
  0.0 2.7 %collective-permute-start = (bf16[1,3,256,128]{3,2,1,0:T(8,128)(2,1)}, bf16[1,3,256,128]{3,2,1,0:T(8,128)(2,1)S(1)}, u32[]{:S(2)}, u32[]{:S(2)}) collective-permute-start(bf16[1,3,256,128]{3,2,1,0:T(8,128)(2,1)} %dens_ref.1), channel_id=1, source_target_pairs={{0,16},{1,17},{2,18},{3,19},{4,20},{5,21},{6,22},{7,23},{8,24},{9,... | collective-permute-start | bytes 589832 | tf_op jit(solution)/shard_map/ppermute | solution.py:47
  2.8 11.5 %collective-permute-start.3 = (bf16[800,128]{1,0:T(8,128)(2,1)S(1)}, bf16[800,128]{1,0:T(8,128)(2,1)S(1)}, u32[]{:S(2)}, u32[]{:S(2)}) collective-permute-start(bf16[800,128]{1,0:T(8,128)(2,1)S(1)} %unit.1), channel_id=1, source_target_pairs={{0,8},{1,9},{2,10},{3,11},{4,12},{5,13},{6,14},{7,15},{8,0},{9,1},... | collective-permute-start | bytes 614408 | tf_op jit(solution)/shard_map/ppermute | solution.py:52
  6.6 7.7 %collective-permute-start.2 = (bf16[800,128]{1,0:T(8,128)(2,1)S(1)}, bf16[800,128]{1,0:T(8,128)(2,1)S(1)}, u32[]{:S(2)}, u32[]{:S(2)}) collective-permute-start(bf16[800,128]{1,0:T(8,128)(2,1)S(1)} %unit.1), channel_id=1, source_target_pairs={{0,12},{1,13},{2,14},{3,15},{4,0},{5,1},{6,2},{7,3},{8,4},{9,5},{1... | collective-permute-start | bytes 614408 | tf_op jit(solution)/shard_map/ppermute | solution.py:52
  7.0 7.3 %collective-permute-start.1 = (bf16[800,128]{1,0:T(8,128)(2,1)S(1)}, bf16[800,128]{1,0:T(8,128)(2,1)S(1)}, u32[]{:S(2)}, u32[]{:S(2)}) collective-permute-start(bf16[800,128]{1,0:T(8,128)(2,1)S(1)} %unit.1), channel_id=1, source_target_pairs={{0,4},{1,5},{2,6},{3,7},{4,8},{5,9},{6,10},{7,11},{8,12},{9,13},{1... | collective-permute-start | bytes 614408 | tf_op jit(solution)/shard_map/ppermute | solution.py:52
  14.4 11.0 %collective-permute-start.5 = (bf16[1600,128]{1,0:T(8,128)(2,1)S(1)}, bf16[1600,128]{1,0:T(8,128)(2,1)S(1)}, u32[]{:S(2)}, u32[]{:S(2)}) collective-permute-start(bf16[1600,128]{1,0:T(8,128)(2,1)S(1)} %constant_dynamic-update-slice_fusion.2.refs_1_), channel_id=1, source_target_pairs={{0,96},{1,97},{2,98},{3,99},{4,100},{5,101},{6,102},{7,103},{8,104... | collective-permute-start | bytes 1228808 | tf_op jit(solution)/shard_map/ppermute | solution.py:57
  17.2 8.4 %collective-permute-start.4 = (bf16[1600,128]{1,0:T(8,128)(2,1)S(1)}, bf16[1600,128]{1,0:T(8,128)(2,1)S(1)}, u32[]{:S(2)}, u32[]{:S(2)}) collective-permute-start(bf16[1600,128]{1,0:T(8,128)(2,1)S(1)} %constant_dynamic-update-slice_fusion.refs_0_), channel_id=1, source_target_pairs={{0,32},{1,33},{2,34},{3,35},{4,36},{5,37},{6,38},{7,39},{8,40},{9,... | collective-permute-start | bytes 1228808 | tf_op jit(solution)/shard_map/ppermute | solution.py:57
  17.3 12.7 %collective-permute-start.6 = (bf16[1600,128]{1,0:T(8,128)(2,1)S(1)}, bf16[1600,128]{1,0:T(8,128)(2,1)S(1)}, u32[]{:S(2)}, u32[]{:S(2)}) collective-permute-start(bf16[1600,128]{1,0:T(8,128)(2,1)S(1)} %constant_dynamic-update-slice_fusion.2.refs_1_), channel_id=1, source_target_pairs={{0,32},{1,33},{2,34},{3,35},{4,36},{5,37},{6,38},{7,39},{8,40},{9,... | collective-permute-start | bytes 1228808 | tf_op jit(solution)/shard_map/ppermute | solution.py:57
  17.4 12.6 %collective-permute-start.7 = (bf16[1600,128]{1,0:T(8,128)(2,1)S(1)}, bf16[1600,128]{1,0:T(8,128)(2,1)S(1)}, u32[]{:S(2)}, u32[]{:S(2)}) collective-permute-start(bf16[1600,128]{1,0:T(8,128)(2,1)S(1)} %constant_dynamic-update-slice_fusion.refs_0_), channel_id=1, source_target_pairs={{0,96},{1,97},{2,98},{3,99},{4,100},{5,101},{6,102},{7,103},{8,104... | collective-permute-start | bytes 1228808 | tf_op jit(solution)/shard_map/ppermute | solution.py:57
  25.6 12.2 %collective-permute-start.8 = (bf16[1600,128]{1,0:T(8,128)(2,1)S(1)}, bf16[1600,128]{1,0:T(8,128)(2,1)S(1)}, u32[]{:S(2)}, u32[]{:S(2)}) collective-permute-start(bf16[1600,128]{1,0:T(8,128)(2,1)S(1)} %collective-permute-done.4.refs_0_), channel_id=1, source_target_pairs={{0,32},{1,33},{2,34},{3,35},{4,36},{5,37},{6,38},{7,39},{8,40},{9,... | collective-permute-start | bytes 1228808 | tf_op jit(solution)/shard_map/ppermute | solution.py:57
  25.6 12.2 %collective-permute-start.9 = (bf16[1600,128]{1,0:T(8,128)(2,1)S(1)}, bf16[1600,128]{1,0:T(8,128)(2,1)S(1)}, u32[]{:S(2)}, u32[]{:S(2)}) collective-permute-start(bf16[1600,128]{1,0:T(8,128)(2,1)S(1)} %collective-permute-done.5.refs_3_), channel_id=1, source_target_pairs={{0,96},{1,97},{2,98},{3,99},{4,100},{5,101},{6,102},{7,103},{8,104... | collective-permute-start | bytes 1228808 | tf_op jit(solution)/shard_map/ppermute | solution.py:57
  41.0 3.2 %collective-permute-start.10 = (bf16[3,800,128]{2,1,0:T(8,128)(2,1)S(1)}, bf16[3,800,128]{2,1,0:T(8,128)(2,1)S(1)}, u32[]{:S(2)}, u32[]{:S(2)}) collective-permute-start(bf16[3,800,128]{2,1,0:T(8,128)(2,1)S(1)} %get-tuple-element.68), channel_id=1, source_target_pairs={{0,16},{1,17},{2,18},{3,19},{4,20},{5,21},{6,22},{7,23},{8,24},{9,... | collective-permute-start | bytes 1843208 | tf_op jit(solution)/shard_map/ppermute | solution.py:47
  44.4 14.4 %copy-start = (bf16[1,32,3,256]{3,1,2,0:T(8,128)(2,1)S(1)}, bf16[1,32,3,256]{3,1,2,0:T(8,128)(2,1)}, u32[]{:S(2)}) copy-start(bf16[1,32,3,256]{3,1,2,0:T(8,128)(2,1)} %param.10) | copy-start | bytes 147460
  44.4 14.0 %collective-permute-start.11 = (bf16[800,128]{1,0:T(8,128)(2,1)S(1)}, bf16[800,128]{1,0:T(8,128)(2,1)S(1)}, u32[]{:S(2)}, u32[]{:S(2)}) collective-permute-start(bf16[800,128]{1,0:T(8,128)(2,1)S(1)} %get-tuple-element.72), channel_id=1, source_target_pairs={{0,2},{1,3},{2,0},{3,1},{4,6},{5,7},{6,4},{7,5},{8,10},{9,11},{10,... | collective-permute-start | bytes 614408 | tf_op jit(solution)/shard_map/ppermute | solution.py:61
  48.7 10.0 %collective-permute-start.12 = (bf16[800,128]{1,0:T(8,128)(2,1)S(1)}, bf16[800,128]{1,0:T(8,128)(2,1)S(1)}, u32[]{:S(2)}, u32[]{:S(2)}) collective-permute-start(bf16[800,128]{1,0:T(8,128)(2,1)S(1)} %get-tuple-element.73), channel_id=1, source_target_pairs={{0,1},{1,2},{2,3},{3,0},{4,5},{5,6},{6,7},{7,4},{8,9},{9,10},{10,1... | collective-permute-start | bytes 614408 | tf_op jit(solution)/shard_map/ppermute | solution.py:61
  48.9 9.8 %collective-permute-start.13 = (bf16[800,128]{1,0:T(8,128)(2,1)S(1)}, bf16[800,128]{1,0:T(8,128)(2,1)S(1)}, u32[]{:S(2)}, u32[]{:S(2)}) collective-permute-start(bf16[800,128]{1,0:T(8,128)(2,1)S(1)} %get-tuple-element.74), channel_id=1, source_target_pairs={{0,3},{1,0},{2,1},{3,2},{4,7},{5,4},{6,5},{7,6},{8,11},{9,8},{10,9... | collective-permute-start | bytes 614408 | tf_op jit(solution)/shard_map/ppermute | solution.py:61

commit v2 on v0

--- a/solution.py
+++ b/solution.py
@@ -273,7 +273,9 @@
             for k in range(4):
                 at = u * 128 + k * RANK
                 wide[at : at + RANK, k * LOADS : (k + 1) * LOADS] = moments
-        coefficients = dot32(blocks[...], wide[...])
+        coefficients = dot32(
+            blocks[:, first_unit * 128 : (first_unit + units) * 128], wide[...]
+        )
         for k in range(4):
             piece = coefficients[:, k * LOADS : (k + 1) * LOADS]
             far[k] = piece if part == "first" else carried_far[k] + piece
@@ -374,7 +376,7 @@
         if part == "own":
             shapes += (jax.ShapeDtypeStruct((2, FULL, LOADS), bf16),)
     else:
-        operands.append(blocks[:, first_unit * 128 : (first_unit + 2 * count) * 128])
+        operands.append(blocks)
         scratch.append(pltpu.VMEM((2 * count * 128, 4 * LOADS), bf16))
         shapes = (sums, far)
         if part == "send":
@@ -466,22 +468,13 @@
     partner = swap_core(densities)
     own, moments, flip = moments_of(core, densities, bases)
     unit = make_unit(core, own, partner, moments)
+    from_across = along_first(unit, 2)
+    from_above = along_first(unit, -1)
     from_below = along_first(unit, 1)
-    from_above = along_first(unit, -1)
-    from_across = along_first(unit, 2)
     here = jnp.stack([z, core, y, x]).astype(jnp.int32)
     here, unit = lax.optimization_barrier((here, unit))
     spread, targets, couplings = make_points(here, positions, areas, couplings)
-    (near_pairs, far_pairs, couplings, spread, targets, unit, from_below, from_above, from_across) = (
-        lax.optimization_barrier(
-            (near_pairs, far_pairs, couplings, spread, targets, unit)
-            + (from_below, from_above, from_across)
-        )
-    )
-    low = jnp.concatenate([unit, from_below], axis=0)
-    high = jnp.concatenate([from_above, from_across], axis=0)
-    low_below = along_second(low, 1)
-    high_above = along_second(high, -1)
+    near_pairs, far_pairs, spread = lax.optimization_barrier((near_pairs, far_pairs, spread))
 
     heads, tails = near_pairs[:, 0], near_pairs[:, 1]
     mark = lambda index, size: index[None, :] == jnp.arange(size, dtype=jnp.int32)[:, None]
@@ -505,9 +498,18 @@
 
     back_cell = jnp.where(far_heads != far_tails, cell(far_tails, far_heads), -1)
     blocks = make_blocks(cell(far_heads, far_tails), back_cell, couplings, flip)
-    blocks, low_later, high_later = lax.optimization_barrier((blocks, low, high))
-    high_below = along_second(high_later, 1)
-    low_above = along_second(low_later, -1)
+    (spread, targets, counts, blocks, unit, from_below, from_above, from_across) = (
+        lax.optimization_barrier(
+            (spread, targets, counts, blocks, unit, from_below, from_above, from_across)
+        )
+    )
+    low = jnp.concatenate([unit, from_below], axis=0)
+    high = jnp.concatenate([from_above, from_across], axis=0)
+    low_below = along_second(low, 1)
+    high_above = along_second(high, -1)
+
+    high_below = along_second(high, 1)
+    low_above = along_second(low, -1)
     tables = (counts, targets, spread)
 
     carried = near("first", 0, (low, high), (), *tables, blocks)

time: 60.2 us -> 59.1 us (0.982)
  starting transfers between devices: 24 us -> 21.6 us
  Pallas kernels: 27.5 us -> 28.3 us
    ppermute x3, starting transfers between devices: 7.55 us -> 4.64 us  [along_z(): lax.ppermute(value, AXES, routes(lambda z, c, y, x: (z + step, c, y, x)))]
    pallas_call x5, Pallas kernels: 19.8 us -> 20.6 us  [near(): pl.pallas_call(functools.partial(near_kernel, first_unit, count, part), o...]
    ppermute x3, waiting for transfers between devices: 0.72 us -> 0.02 us  [along_first(): return lax.ppermute(value, AXES, routes(move))]
    ppermute x3, waiting for transfers between devices: 0.01 us -> 0.69 us  [along_z(): lax.ppermute(value, AXES, routes(lambda z, c, y, x: (z + step, c, y, x)))]
  transfers between devices with their start and end apart: 14 -> 14, of which waited for: 4 -> 4; matrix products, arithmetic and copies ran while one was open for 1% -> 1% of each run, Pallas kernels for 39% -> 41%
where the time goes in v2:
time: 59.1 us; the launch traced here: 59 us
  Pallas kernels  28.3 us (48%)
  starting transfers between devices  21.6 us (37%)
  blocking collectives  4.67 us (8%)
  waiting for transfers between devices  3.32 us (6%)
  other arithmetic  0.64 us (1%)
    pallas_call x5, Pallas kernels, near(): pl.pallas_call(functools.partial(near_kernel, first_unit, count, part), o...  20.6 us
    ppermute x6, starting transfers between devices, along_second(): return lax.ppermute(value, AXES, routes(move))  8.04 us
    all_to_all x1, blocking collectives, local(): lax.all_to_all(pair, 'row', 0, 0, axis_index_groups=chips, tiled=True)  4.67 us
    ppermute x3, starting transfers between devices, along_z(): lax.ppermute(value, AXES, routes(lambda z, c, y, x: (z + step, c, y, x)))  4.64 us
    pallas_call x1, Pallas kernels, make_points(): pl.pallas_call(points_kernel, out_shape=(jax.ShapeDtypeStruct((32, 4, HAL...  4.6 us
    ppermute x3, starting transfers between devices, along_first(): return lax.ppermute(value, AXES, routes(move))  4.54 us
    ppermute x2, starting transfers between devices, swap_core(): lax.ppermute(value, AXES, routes(lambda z, c, y, x: (z, 1 - c, y, x)))  4.33 us
    ppermute x6, waiting for transfers between devices, along_second(): return lax.ppermute(value, AXES, routes(move))  2.54 us
  transfers between devices with their start and end apart: 14, of which 4 were waited for; matrix products, arithmetic and copies ran while one was open for 1% of the time, Pallas kernels for 41%

profile of v2, /device:TPU:1, one launch (start us, length us, event | category | flops | bytes accessed | tf_op | source)
XLA Modules:
  0.0 59.0 jit_solution(9237614027831708128)
XLA Ops:
  0.0 1.4 %collective-permute-start = (bf16[1,3,256,128]{3,2,1,0:T(8,128)(2,1)}, bf16[1,3,256,128]{3,2,1,0:T(8,128)(2,1)S(1)}, u32[]{:S(2)}, u32[]{:S(2)}) collective-permute-start(bf16[1,3,256,128]{3,2,1,0:T(8,128)(2,1)} %dens_ref.1), channel_id=1, source_target_pairs={{0,16},{1,17},{2,18},{3,19},{4,20},{5,21},{6,22},{7,23},{8,24},{9,... | collective-permute-start | bytes 589832 | tf_op jit(solution)/shard_map/ppermute | solution.py:46
  1.4 1.1 %moments.1 = (bf16[384,128]{1,0:T(8,128)(2,1)S(1)}, bf16[32,128]{1,0:T(8,128)(2,1)S(1)}, bf16[1024,1024]{1,0:T(8,128)(2,1)S(1)}) custom-call(s32[1]{0:T(128)} %bitcast.core_ref.core, bf16[1,3,256,128]{3,2,1,0:T(8,128)(2,1)} %dens_ref.1, bf16[1,3,32,256]{3,2,1,0:T(8,128)(2,1)} %bitcast.68), custom_call_target="tpu_custom_call" | custom-call | tf_op jit(solution)/shard_map/moments/pallas_call | solution.py:105
  2.6 0.1 pad_add_fusion.2.here_ref
  2.6 0.1 collective-permute-done.partner_ref
  2.7 0.1 unit.1
  2.8 3.1 %collective-permute-start.3 = (bf16[800,128]{1,0:T(8,128)(2,1)S(1)}, bf16[800,128]{1,0:T(8,128)(2,1)S(1)}, u32[]{:S(2)}, u32[]{:S(2)}) collective-permute-start(bf16[800,128]{1,0:T(8,128)(2,1)S(1)} %unit.1), channel_id=1, source_target_pairs={{0,2},{1,3},{2,0},{3,1},{4,6},{5,7},{6,4},{7,5},{8,10},{9,11},{10,... | collective-permute-start | bytes 614408 | tf_op jit(solution)/shard_map/ppermute | solution.py:51
  5.9 0.8 %collective-permute-start.2 = (bf16[800,128]{1,0:T(8,128)(2,1)S(1)}, bf16[800,128]{1,0:T(8,128)(2,1)S(1)}, u32[]{:S(2)}, u32[]{:S(2)}) collective-permute-start(bf16[800,128]{1,0:T(8,128)(2,1)S(1)} %unit.1), channel_id=1, source_target_pairs={{0,3},{1,0},{2,1},{3,2},{4,7},{5,4},{6,5},{7,6},{8,11},{9,8},{10,9... | collective-permute-start | bytes 614408 | tf_op jit(solution)/shard_map/ppermute | solution.py:51
  6.7 0.7 %collective-permute-start.1 = (bf16[800,128]{1,0:T(8,128)(2,1)S(1)}, bf16[800,128]{1,0:T(8,128)(2,1)S(1)}, u32[]{:S(2)}, u32[]{:S(2)}) collective-permute-start(bf16[800,128]{1,0:T(8,128)(2,1)S(1)} %unit.1), channel_id=1, source_target_pairs={{0,1},{1,2},{2,3},{3,0},{4,5},{5,6},{6,7},{7,4},{8,9},{9,10},{10,1... | collective-permute-start | bytes 614408 | tf_op jit(solution)/shard_map/ppermute | solution.py:51
  7.3 4.6 %points.1 = (f32[32,4,128,128]{3,2,1,0:T(8,128)S(1)}, f32[8,8,256]{2,1,0:T(8,128)S(1)}, bf16[768,1024]{1,0:T(8,128)(2,1)S(1)}) custom-call(s32[4]{0:T(128)S(1)} %pad_add_fusion.2.here_ref, f32[3,128,256]{2,1,0:T(8,128)} %bitcast.70, f32[128,256]{1,0:T(8,128)} %areas_ref.1, bf16[768,1024]{1,0:T(8,128)(2,1)} %couplings_ref.1), custom_call_target="tpu_custom_call" | custom-call | tf_op jit(solution)/shard_map/points/pallas_call | solution.py:177
  11.9 0.0 copy-done.1
  12.0 0.1 compare_reduce_fusion.2
  12.0 0.2 fusion.27
  12.3 0.0 copy-done.2
  12.3 0.1 bitcast_select_fusion.1
  12.4 0.9 %coupling_blocks.1.refs_2_.refs_4_ = bf16[64,2048]{1,0:T(8,128)(2,1)S(1)} custom-call(s32[1,768]{1,0:T(1,128)S(1)} %get-tuple-element.86.forward_ref, s32[1,768]{1,0:T(1,128)S(1)} %get-tuple-element.85.backward_ref, bf16[768,1024]{1,0:T(8,128)(2,1)S(1)} %get-tuple-element.48.couplings_ref, bf16[1024,1024]{1,0:T(8,128)(2,1)S(1)} %get-tuple-element.49.flip_ref), custom_call_target="tpu_custom_call" | custom-call | tf_op jit(solution)/shard_map/coupling_blocks/pallas_call | solution.py:215
  13.4 0.2 fusion.2.counts
  13.6 0.0 collective-permute-done.3
  13.6 0.0 collective-permute-done.2
  13.6 0.0 collective-permute-done.1
  13.7 2.5 %collective-permute-start.5 = (bf16[1600,128]{1,0:T(8,128)(2,1)S(1)}, bf16[1600,128]{1,0:T(8,128)(2,1)S(1)}, u32[]{:S(2)}, u32[]{:S(2)}) collective-permute-start(bf16[1600,128]{1,0:T(8,128)(2,1)S(1)} %constant_dynamic-update-slice_fusion.2.refs_1_), channel_id=1, source_target_pairs={{0,12},{1,13},{2,14},{3,15},{4,0},{5,1},{6,2},{7,3},{8,4},{9,5},{1... | collective-permute-start | bytes 1228808 | tf_op jit(solution)/shard_map/ppermute | solution.py:56
  16.2 0.1 collective-permute-start.4
  16.3 0.2 collective-permute-start.6
  16.5 2.6 %collective-permute-start.7 = (bf16[1600,128]{1,0:T(8,128)(2,1)S(1)}, bf16[1600,128]{1,0:T(8,128)(2,1)S(1)}, u32[]{:S(2)}, u32[]{:S(2)}) collective-permute-start(bf16[1600,128]{1,0:T(8,128)(2,1)S(1)} %constant_dynamic-update-slice_fusion.refs_0_), channel_id=1, source_target_pairs={{0,12},{1,13},{2,14},{3,15},{4,0},{5,1},{6,2},{7,3},{8,4},{9,5},{1... | collective-permute-start | bytes 1228808 | tf_op jit(solution)/shard_map/ppermute | solution.py:56
  19.1 4.7 %near_first.1 = (f32[6,768,128]{2,1,0:T(8,128)S(1)}, f32[4,64,128]{2,1,0:T(8,128)S(1)}) custom-call(s32[8,32]{1,0:T(8,128)S(1)} %fusion.2.counts, f32[8,8,256]{2,1,0:T(8,128)S(1)} %get-tuple-element.52.targets, f32[32,4,128,128]{3,2,1,0:T(8,128)S(1)} %get-tuple-element.53.spread, bf16[1600,128]{1,0:T(8,128)(2,1)S(1)} %constant_dynamic-update-slice_fusion.refs_0_, ...), custom_call_target="tpu_custom_call" | custom-call | flops 2000000000 | bytes 8000000 | tf_op jit(solution)/shard_map/near_first/pallas_call | solution.py:386
  23.8 0.0 collective-permute-done.5.refs_3_.refs_5_
  23.8 0.8 %collective-permute-done.4.refs_0_.refs_2_ = bf16[1600,128]{1,0:T(8,128)(2,1)S(1)} collective-permute-done((bf16[1600,128]{1,0:T(8,128)(2,1)S(1)}, bf16[1600,128]{1,0:T(8,128)(2,1)S(1)}, u32[]{:S(2)}, u32[]{:S(2)}) %collective-permute-start.4) | collective-permute-done | bytes 409632 | tf_op jit(solution)/shard_map/ppermute | solution.py:56
  24.6 0.0 collective-permute-start.8
  24.6 2.7 %collective-permute-start.9 = (bf16[1600,128]{1,0:T(8,128)(2,1)S(1)}, bf16[1600,128]{1,0:T(8,128)(2,1)S(1)}, u32[]{:S(2)}, u32[]{:S(2)}) collective-permute-start(bf16[1600,128]{1,0:T(8,128)(2,1)S(1)} %collective-permute-done.5.refs_3_.refs_5_), channel_id=1, source_target_pairs={{0,12},{1,13},{2,14},{3,15},{4,0},{5,1},{6,2},{7,3},{8,4},{9,5},{1... | collective-permute-start | bytes 1228808 | tf_op jit(solution)/shard_map/ppermute | solution.py:56
  27.3 1.7 %collective-permute-done.6.refs_1_.refs_3_ = bf16[1600,128]{1,0:T(8,128)(2,1)S(1)} collective-permute-done((bf16[1600,128]{1,0:T(8,128)(2,1)S(1)}, bf16[1600,128]{1,0:T(8,128)(2,1)S(1)}, u32[]{:S(2)}, u32[]{:S(2)}) %collective-permute-start.6) | collective-permute-done | bytes 409632 | tf_op jit(solution)/shard_map/ppermute | solution.py:56
  29.0 0.0 collective-permute-done.7.refs_2_.refs_4_
  29.0 6.1 %near_middle.1 = (f32[6,768,128]{2,1,0:T(8,128)S(1)}, f32[4,64,128]{2,1,0:T(8,128)S(1)}) custom-call(s32[8,32]{1,0:T(8,128)S(1)} %fusion.2.counts, f32[8,8,256]{2,1,0:T(8,128)S(1)} %get-tuple-element.52.targets, f32[32,4,128,128]{3,2,1,0:T(8,128)S(1)} %get-tuple-element.53.spread, bf16[1600,128]{1,0:T(8,128)(2,1)S(1)} %collective-permute-done.4.refs_0_.refs_2_, ...), custom_call_target="tpu_custom_call" | custom-call | flops 4000000000 | bytes 8000000 | tf_op jit(solution)/shard_map/near_middle/pallas_call | solution.py:386
  35.1 0.0 collective-permute-done.8.refs_0_.refs_6_
  35.2 0.0 collective-permute-done.9.refs_1_.refs_7_
  35.2 3.2 %near_send.1 = (bf16[3,800,128]{2,1,0:T(8,128)(2,1)S(1)}, f32[4,64,128]{2,1,0:T(8,128)S(1)}) custom-call(s32[8,32]{1,0:T(8,128)S(1)} %fusion.2.counts, f32[8,8,256]{2,1,0:T(8,128)S(1)} %get-tuple-element.52.targets, f32[32,4,128,128]{3,2,1,0:T(8,128)S(1)} %get-tuple-element.53.spread, bf16[1600,128]{1,0:T(8,128)(2,1)S(1)} %collective-permute-done.8.refs_0_.refs_6_, ...), custom_call_target="tpu_custom_call" | custom-call | flops 2000000000 | bytes 8000000 | tf_op jit(solution)/shard_map/near_send/pallas_call | solution.py:386
  38.4 2.9 %collective-permute-start.10 = (bf16[3,800,128]{2,1,0:T(8,128)(2,1)S(1)}, bf16[3,800,128]{2,1,0:T(8,128)(2,1)S(1)}, u32[]{:S(2)}, u32[]{:S(2)}) collective-permute-start(bf16[3,800,128]{2,1,0:T(8,128)(2,1)S(1)} %get-tuple-element.68), channel_id=1, source_target_pairs={{0,16},{1,17},{2,18},{3,19},{4,20},{5,21},{6,22},{7,23},{8,24},{9,... | collective-permute-start | bytes 1843208 | tf_op jit(solution)/shard_map/ppermute | solution.py:46
  41.3 2.7 %near_keep.1 = f32[3,800,128]{2,1,0:T(8,128)S(1)} custom-call(s32[8,32]{1,0:T(8,128)S(1)} %fusion.2.counts, f32[8,8,256]{2,1,0:T(8,128)S(1)} %get-tuple-element.52.targets, f32[32,4,128,128]{3,2,1,0:T(8,128)S(1)} %get-tuple-element.53.spread, bf16[1600,128]{1,0:T(8,128)(2,1)S(1)} %collective-permute-done.8.refs_0_.refs_6_, ...), custom_call_target="tpu_custom_call" | custom-call | flops 2000000000 | bytes 8000000 | tf_op jit(solution)/shard_map/near_keep/pallas_call | solution.py:386
  44.0 0.0 collective-permute-done.10
  44.0 0.1 fusion.9
  44.2 0.0 copy-start
  44.2 1.7 %collective-permute-start.11 = (bf16[800,128]{1,0:T(8,128)(2,1)S(1)}, bf16[800,128]{1,0:T(8,128)(2,1)S(1)}, u32[]{:S(2)}, u32[]{:S(2)}) collective-permute-start(bf16[800,128]{1,0:T(8,128)(2,1)S(1)} %get-tuple-element.72), channel_id=1, source_target_pairs={{0,32},{1,33},{2,34},{3,35},{4,36},{5,37},{6,38},{7,39},{8,40},{9,... | collective-permute-start | bytes 614408 | tf_op jit(solution)/shard_map/ppermute | solution.py:60
  45.9 1.8 %collective-permute-start.12 = (bf16[800,128]{1,0:T(8,128)(2,1)S(1)}, bf16[800,128]{1,0:T(8,128)(2,1)S(1)}, u32[]{:S(2)}, u32[]{:S(2)}) collective-permute-start(bf16[800,128]{1,0:T(8,128)(2,1)S(1)} %get-tuple-element.73), channel_id=1, source_target_pairs={{0,96},{1,97},{2,98},{3,99},{4,100},{5,101},{6,102},{7,103},{8,104... | collective-permute-start | bytes 614408 | tf_op jit(solution)/shard_map/ppermute | solution.py:60
  47.7 1.1 %collective-permute-start.13 = (bf16[800,128]{1,0:T(8,128)(2,1)S(1)}, bf16[800,128]{1,0:T(8,128)(2,1)S(1)}, u32[]{:S(2)}, u32[]{:S(2)}) collective-permute-start(bf16[800,128]{1,0:T(8,128)(2,1)S(1)} %get-tuple-element.74), channel_id=1, source_target_pairs={{0,64},{1,65},{2,66},{3,67},{4,68},{5,69},{6,70},{7,71},{8,72},{9,... | collective-permute-start | bytes 614408 | tf_op jit(solution)/shard_map/ppermute | solution.py:60
  48.8 3.8 %near_own.1 = (f32[2,800,128]{2,1,0:T(8,128)S(1)}, bf16[2,800,128]{2,1,0:T(8,128)(2,1)S(1)}) custom-call(s32[8,32]{1,0:T(8,128)S(1)} %fusion.2.counts, f32[8,8,256]{2,1,0:T(8,128)S(1)} %get-tuple-element.52.targets, f32[32,4,128,128]{3,2,1,0:T(8,128)S(1)} %get-tuple-element.53.spread, bf16[1600,128]{1,0:T(8,128)(2,1)S(1)} %constant_dynamic-update-slice_fusion.refs_0_, ...), custom_call_target="tpu_custom_call" | custom-call | flops 8000000000 | bytes 8000000 | tf_op jit(solution)/shard_map/near_own/pallas_call | solution.py:386
  52.6 4.7 %all_to_all.5.swapped = bf16[2,800,128]{2,1,0:T(8,128)(2,1)S(1)} all-to-all(bf16[2,800,128]{2,1,0:T(8,128)(2,1)S(1)} %get-tuple-element.71), channel_id=1, replica_groups={{0,16},{32,48},{64,80},{96,112},{1,17},{33,49},{65,81},{97,113},{2,18},..., dimensions={0} | all-to-all | bytes 819200 | tf_op jit(solution)/shard_map/all_to_all | solution.py:532
  57.3 0.0 collective-permute-done.11.one
  57.3 0.0 collective-permute-done.12.two
  57.3 0.7 %collective-permute-done.13.three = bf16[800,128]{1,0:T(8,128)(2,1)S(1)} collective-permute-done((bf16[800,128]{1,0:T(8,128)(2,1)S(1)}, bf16[800,128]{1,0:T(8,128)(2,1)S(1)}, u32[]{:S(2)}, u32[]{:S(2)}) %collective-permute-start.13) | collective-permute-done | bytes 204832 | tf_op jit(solution)/shard_map/ppermute | solution.py:60
  58.0 1.0 %sum_and_expand.1 = bf16[1,3,256,128]{3,2,1,0:T(8,128)(2,1)} custom-call(s32[1]{0:T(128)} %bitcast.core_ref.core, f32[2,800,128]{2,1,0:T(8,128)S(1)} %get-tuple-element.70.keep, bf16[2,800,128]{2,1,0:T(8,128)(2,1)S(1)} %all_to_all.5.swapped, bf16[800,128]{1,0:T(8,128)(2,1)S(1)} %collective-permute-done.11.one, ...), custom_call_target="tpu_custom_call" | custom-call | tf_op jit(solution)/shard_map/sum_and_expand/pallas_call | solution.py:429
  (11 shorter events, 0.1 us)
Async XLA Ops:
  0.0 12.3 %copy-start.2 = (s32[768,2]{0,1:T(2,128)S(1)}, s32[768,2]{0,1:T(2,128)}, u32[]{:S(2)}) copy-start(s32[768,2]{0,1:T(2,128)} %param.12) | copy-start | bytes 18436
  0.0 11.9 %copy-start.1 = (s32[1920,2]{0,1:T(2,128)S(1)}, s32[1920,2]{0,1:T(2,128)}, u32[]{:S(2)}) copy-start(s32[1920,2]{0,1:T(2,128)} %param.11) | copy-start | bytes 46084
  0.0 2.7 %collective-permute-start = (bf16[1,3,256,128]{3,2,1,0:T(8,128)(2,1)}, bf16[1,3,256,128]{3,2,1,0:T(8,128)(2,1)S(1)}, u32[]{:S(2)}, u32[]{:S(2)}) collective-permute-start(bf16[1,3,256,128]{3,2,1,0:T(8,128)(2,1)} %dens_ref.1), channel_id=1, source_target_pairs={{0,16},{1,17},{2,18},{3,19},{4,20},{5,21},{6,22},{7,23},{8,24},{9,... | collective-permute-start | bytes 589832 | tf_op jit(solution)/shard_map/ppermute | solution.py:46
  2.8 10.8 %collective-permute-start.3 = (bf16[800,128]{1,0:T(8,128)(2,1)S(1)}, bf16[800,128]{1,0:T(8,128)(2,1)S(1)}, u32[]{:S(2)}, u32[]{:S(2)}) collective-permute-start(bf16[800,128]{1,0:T(8,128)(2,1)S(1)} %unit.1), channel_id=1, source_target_pairs={{0,2},{1,3},{2,0},{3,1},{4,6},{5,7},{6,4},{7,5},{8,10},{9,11},{10,... | collective-permute-start | bytes 614408 | tf_op jit(solution)/shard_map/ppermute | solution.py:51
  5.9 7.7 %collective-permute-start.2 = (bf16[800,128]{1,0:T(8,128)(2,1)S(1)}, bf16[800,128]{1,0:T(8,128)(2,1)S(1)}, u32[]{:S(2)}, u32[]{:S(2)}) collective-permute-start(bf16[800,128]{1,0:T(8,128)(2,1)S(1)} %unit.1), channel_id=1, source_target_pairs={{0,3},{1,0},{2,1},{3,2},{4,7},{5,4},{6,5},{7,6},{8,11},{9,8},{10,9... | collective-permute-start | bytes 614408 | tf_op jit(solution)/shard_map/ppermute | solution.py:51
  6.7 6.9 %collective-permute-start.1 = (bf16[800,128]{1,0:T(8,128)(2,1)S(1)}, bf16[800,128]{1,0:T(8,128)(2,1)S(1)}, u32[]{:S(2)}, u32[]{:S(2)}) collective-permute-start(bf16[800,128]{1,0:T(8,128)(2,1)S(1)} %unit.1), channel_id=1, source_target_pairs={{0,1},{1,2},{2,3},{3,0},{4,5},{5,6},{6,7},{7,4},{8,9},{9,10},{10,1... | collective-permute-start | bytes 614408 | tf_op jit(solution)/shard_map/ppermute | solution.py:51
  13.7 10.1 %collective-permute-start.5 = (bf16[1600,128]{1,0:T(8,128)(2,1)S(1)}, bf16[1600,128]{1,0:T(8,128)(2,1)S(1)}, u32[]{:S(2)}, u32[]{:S(2)}) collective-permute-start(bf16[1600,128]{1,0:T(8,128)(2,1)S(1)} %constant_dynamic-update-slice_fusion.2.refs_1_), channel_id=1, source_target_pairs={{0,12},{1,13},{2,14},{3,15},{4,0},{5,1},{6,2},{7,3},{8,4},{9,5},{1... | collective-permute-start | bytes 1228808 | tf_op jit(solution)/shard_map/ppermute | solution.py:56
  16.2 8.4 %collective-permute-start.4 = (bf16[1600,128]{1,0:T(8,128)(2,1)S(1)}, bf16[1600,128]{1,0:T(8,128)(2,1)S(1)}, u32[]{:S(2)}, u32[]{:S(2)}) collective-permute-start(bf16[1600,128]{1,0:T(8,128)(2,1)S(1)} %constant_dynamic-update-slice_fusion.refs_0_), channel_id=1, source_target_pairs={{0,4},{1,5},{2,6},{3,7},{4,8},{5,9},{6,10},{7,11},{8,12},{9,13},{1... | collective-permute-start | bytes 1228808 | tf_op jit(solution)/shard_map/ppermute | solution.py:56
  16.3 12.7 %collective-permute-start.6 = (bf16[1600,128]{1,0:T(8,128)(2,1)S(1)}, bf16[1600,128]{1,0:T(8,128)(2,1)S(1)}, u32[]{:S(2)}, u32[]{:S(2)}) collective-permute-start(bf16[1600,128]{1,0:T(8,128)(2,1)S(1)} %constant_dynamic-update-slice_fusion.2.refs_1_), channel_id=1, source_target_pairs={{0,4},{1,5},{2,6},{3,7},{4,8},{5,9},{6,10},{7,11},{8,12},{9,13},{1... | collective-permute-start | bytes 1228808 | tf_op jit(solution)/shard_map/ppermute | solution.py:56
  16.5 12.5 %collective-permute-start.7 = (bf16[1600,128]{1,0:T(8,128)(2,1)S(1)}, bf16[1600,128]{1,0:T(8,128)(2,1)S(1)}, u32[]{:S(2)}, u32[]{:S(2)}) collective-permute-start(bf16[1600,128]{1,0:T(8,128)(2,1)S(1)} %constant_dynamic-update-slice_fusion.refs_0_), channel_id=1, source_target_pairs={{0,12},{1,13},{2,14},{3,15},{4,0},{5,1},{6,2},{7,3},{8,4},{9,5},{1... | collective-permute-start | bytes 1228808 | tf_op jit(solution)/shard_map/ppermute | solution.py:56
  24.6 10.5 %collective-permute-start.8 = (bf16[1600,128]{1,0:T(8,128)(2,1)S(1)}, bf16[1600,128]{1,0:T(8,128)(2,1)S(1)}, u32[]{:S(2)}, u32[]{:S(2)}) collective-permute-start(bf16[1600,128]{1,0:T(8,128)(2,1)S(1)} %collective-permute-done.4.refs_0_.refs_2_), channel_id=1, source_target_pairs={{0,4},{1,5},{2,6},{3,7},{4,8},{5,9},{6,10},{7,11},{8,12},{9,13},{1... | collective-permute-start | bytes 1228808 | tf_op jit(solution)/shard_map/ppermute | solution.py:56
  24.6 10.5 %collective-permute-start.9 = (bf16[1600,128]{1,0:T(8,128)(2,1)S(1)}, bf16[1600,128]{1,0:T(8,128)(2,1)S(1)}, u32[]{:S(2)}, u32[]{:S(2)}) collective-permute-start(bf16[1600,128]{1,0:T(8,128)(2,1)S(1)} %collective-permute-done.5.refs_3_.refs_5_), channel_id=1, source_target_pairs={{0,12},{1,13},{2,14},{3,15},{4,0},{5,1},{6,2},{7,3},{8,4},{9,5},{1... | collective-permute-start | bytes 1228808 | tf_op jit(solution)/shard_map/ppermute | solution.py:56
  38.4 5.7 %collective-permute-start.10 = (bf16[3,800,128]{2,1,0:T(8,128)(2,1)S(1)}, bf16[3,800,128]{2,1,0:T(8,128)(2,1)S(1)}, u32[]{:S(2)}, u32[]{:S(2)}) collective-permute-start(bf16[3,800,128]{2,1,0:T(8,128)(2,1)S(1)} %get-tuple-element.68), channel_id=1, source_target_pairs={{0,16},{1,17},{2,18},{3,19},{4,20},{5,21},{6,22},{7,23},{8,24},{9,... | collective-permute-start | bytes 1843208 | tf_op jit(solution)/shard_map/ppermute | solution.py:46
  44.2 13.8 %copy-start = (bf16[1,32,3,256]{3,1,2,0:T(8,128)(2,1)S(1)}, bf16[1,32,3,256]{3,1,2,0:T(8,128)(2,1)}, u32[]{:S(2)}) copy-start(bf16[1,32,3,256]{3,1,2,0:T(8,128)(2,1)} %param.10) | copy-start | bytes 147460
  44.2 13.1 %collective-permute-start.11 = (bf16[800,128]{1,0:T(8,128)(2,1)S(1)}, bf16[800,128]{1,0:T(8,128)(2,1)S(1)}, u32[]{:S(2)}, u32[]{:S(2)}) collective-permute-start(bf16[800,128]{1,0:T(8,128)(2,1)S(1)} %get-tuple-element.72), channel_id=1, source_target_pairs={{0,32},{1,33},{2,34},{3,35},{4,36},{5,37},{6,38},{7,39},{8,40},{9,... | collective-permute-start | bytes 614408 | tf_op jit(solution)/shard_map/ppermute | solution.py:60
  45.9 11.4 %collective-permute-start.12 = (bf16[800,128]{1,0:T(8,128)(2,1)S(1)}, bf16[800,128]{1,0:T(8,128)(2,1)S(1)}, u32[]{:S(2)}, u32[]{:S(2)}) collective-permute-start(bf16[800,128]{1,0:T(8,128)(2,1)S(1)} %get-tuple-element.73), channel_id=1, source_target_pairs={{0,96},{1,97},{2,98},{3,99},{4,100},{5,101},{6,102},{7,103},{8,104... | collective-permute-start | bytes 614408 | tf_op jit(solution)/shard_map/ppermute | solution.py:60
  47.7 10.3 %collective-permute-start.13 = (bf16[800,128]{1,0:T(8,128)(2,1)S(1)}, bf16[800,128]{1,0:T(8,128)(2,1)S(1)}, u32[]{:S(2)}, u32[]{:S(2)}) collective-permute-start(bf16[800,128]{1,0:T(8,128)(2,1)S(1)} %get-tuple-element.74), channel_id=1, source_target_pairs={{0,64},{1,65},{2,66},{3,67},{4,68},{5,69},{6,70},{7,71},{8,72},{9,... | collective-permute-start | bytes 614408 | tf_op jit(solution)/shard_map/ppermute | solution.py:60

commit v3 on v0

--- a/solution.py
+++ b/solution.py
@@ -18,7 +18,7 @@
 AXES = ("row", "col")
 TARGETS = ((1, 0), (2, 0), (3, 0), (1, 1), (2, 1), (3, 1), (0, 0), (0, 1))
 AWAY = 6
-SPANS = {"first": (0, AWAY), "middle": (0, AWAY), "send": (3, AWAY), "keep": (0, 3), "own": (AWAY, 8)}
+SPANS = {"first": (0, 8), "middle": (0, AWAY), "send": (3, AWAY), "keep": (0, 3), "own": (AWAY, 8)}
 SIDE = 4
 
 eps_square = 0.0004
@@ -235,7 +235,7 @@
     elif part == "keep":
         carried, far, refs = refs[0], refs[1], refs[2:]
     elif part == "own":
-        far, refs = refs[0], refs[1:]
+        carried, far, refs = refs[0], refs[1], refs[2:]
     if part == "send":
         send, far, acc, refs = refs[0], refs[1], refs[2], refs[3:]
     elif sums_far:
@@ -260,7 +260,7 @@
     for k in range(6):
         entry[entries + k] = low * 64 + 2 * first_unit
     near_rows = slice(0, 3 * CS)
-    if part in ("first", "own"):
+    if part == "first":
         acc[:, near_rows] = jnp.zeros((high - low, 3 * CS, LOADS), f32)
     else:
         acc[:, near_rows] = carried[low:high]
@@ -359,7 +359,7 @@
 def near(part, first_unit, buffers, carried, counts, targets, spread, blocks):
     count = len(buffers)
     slots = 4 * count
-    sums = jax.ShapeDtypeStruct((AWAY, 3 * CS, LOADS), f32)
+    sums = jax.ShapeDtypeStruct((SPANS[part][1], 3 * CS, LOADS), f32)
     far = jax.ShapeDtypeStruct((4, 64, LOADS), f32)
     scratch = [
         pltpu.VMEM((count * 2 * UNIT, LOADS), bf16),
@@ -511,6 +511,7 @@
     tables = (counts, targets, spread)
 
     carried = near("first", 0, (low, high), (), *tables, blocks)
+    started = carried[0]
     low_below, high_above, carried = lax.optimization_barrier((low_below, high_above, carried))
     low_across = along_second(low_below, 1)
     high_across = along_second(high_above, -1)
@@ -524,8 +525,7 @@
     both, far = lax.optimization_barrier((both, far))
     others = [along_z(both[0], 1), along_z(both[2], 3)]
     others.append(along_z(both[1], 2))
-    everything = (low, high) + beside + across
-    own, pair = near("own", 0, everything, (far,), *tables, blocks)
+    own, pair = near("own", 4, beside + across, (started, far), *tables, blocks)
     chips = [[2 * k, 2 * k + 1] for k in range(SIDE)]
     swapped = lax.all_to_all(pair, "row", 0, 0, axis_index_groups=chips, tiled=True)
     return finish(core, own, swapped, others, bases)

time: 60.2 us -> 60.8 us (level)
  blocking collectives: 4.58 us -> 3.67 us
  starting transfers between devices: 24 us -> 24.8 us
  waiting for transfers between devices: 2.94 us -> 3.57 us
    ppermute x3, waiting for transfers between devices: 0.01 us -> 2.43 us  [along_z(): lax.ppermute(value, AXES, routes(lambda z, c, y, x: (z + step, c, y, x)))]
    ppermute x2, starting transfers between devices: 4.13 us -> 6.3 us  [swap_core(): lax.ppermute(value, AXES, routes(lambda z, c, y, x: (z, 1 - c, y, x)))]
    ppermute x6, waiting for transfers between devices: 2.05 us -> 0.25 us  [along_second(): return lax.ppermute(value, AXES, routes(move))]
    ppermute x3, starting transfers between devices: 7.55 us -> 6.07 us  [along_z(): lax.ppermute(value, AXES, routes(lambda z, c, y, x: (z + step, c, y, x)))]
    all_to_all x1, blocking collectives: 4.58 us -> 3.67 us  [local(): lax.all_to_all(pair, 'row', 0, 0, axis_index_groups=chips, tiled=True)]
  transfers between devices with their start and end apart: 14 -> 14, of which waited for: 4 -> 5; matrix products, arithmetic and copies ran while one was open for 1% -> 1% of each run, Pallas kernels for 39% -> 39%
where the time goes in v3:
time: 60.8 us; the launch traced here: 61.2 us
  Pallas kernels  28 us (46%)
  starting transfers between devices  24.8 us (41%)
  blocking collectives  3.67 us (6%)
  waiting for transfers between devices  3.57 us (6%)
  other arithmetic  0.63 us (1%)
    pallas_call x5, Pallas kernels, near(): pl.pallas_call(functools.partial(near_kernel, first_unit, count, part), o...  20.3 us
    ppermute x6, starting transfers between devices, along_second(): return lax.ppermute(value, AXES, routes(move))  7.88 us
    ppermute x2, starting transfers between devices, swap_core(): lax.ppermute(value, AXES, routes(lambda z, c, y, x: (z, 1 - c, y, x)))  6.3 us
    ppermute x3, starting transfers between devices, along_z(): lax.ppermute(value, AXES, routes(lambda z, c, y, x: (z + step, c, y, x)))  6.07 us
    pallas_call x1, Pallas kernels, make_points(): pl.pallas_call(points_kernel, out_shape=(jax.ShapeDtypeStruct((32, 4, HAL...  4.6 us
    ppermute x3, starting transfers between devices, along_first(): return lax.ppermute(value, AXES, routes(move))  4.54 us
    all_to_all x1, blocking collectives, local(): lax.all_to_all(pair, 'row', 0, 0, axis_index_groups=chips, tiled=True)  3.67 us
    ppermute x3, waiting for transfers between devices, along_z(): lax.ppermute(value, AXES, routes(lambda z, c, y, x: (z + step, c, y, x)))  2.43 us
  transfers between devices with their start and end apart: 14, of which 5 were waited for; matrix products, arithmetic and copies ran while one was open for 1% of the time, Pallas kernels for 39%

profile of v3, /device:TPU:1, one launch (start us, length us, event | category | flops | bytes accessed | tf_op | source)
XLA Modules:
  0.0 61.2 jit_solution(16961972019436144356)
XLA Ops:
  0.0 1.4 %collective-permute-start = (bf16[1,3,256,128]{3,2,1,0:T(8,128)(2,1)}, bf16[1,3,256,128]{3,2,1,0:T(8,128)(2,1)S(1)}, u32[]{:S(2)}, u32[]{:S(2)}) collective-permute-start(bf16[1,3,256,128]{3,2,1,0:T(8,128)(2,1)} %dens_ref.1), channel_id=1, source_target_pairs={{0,16},{1,17},{2,18},{3,19},{4,20},{5,21},{6,22},{7,23},{8,24},{9,... | collective-permute-start | bytes 589832 | tf_op jit(solution)/shard_map/ppermute | solution.py:46
  1.4 1.1 %moments.1 = (bf16[384,128]{1,0:T(8,128)(2,1)S(1)}, bf16[32,128]{1,0:T(8,128)(2,1)S(1)}, bf16[1024,1024]{1,0:T(8,128)(2,1)S(1)}) custom-call(s32[1]{0:T(128)} %bitcast.core_ref.core, bf16[1,3,256,128]{3,2,1,0:T(8,128)(2,1)} %dens_ref.1, bf16[1,3,32,256]{3,2,1,0:T(8,128)(2,1)} %bitcast.68), custom_call_target="tpu_custom_call" | custom-call | tf_op jit(solution)/shard_map/moments/pallas_call | solution.py:105
  2.5 0.2 collective-permute-done.partner_ref
  2.7 0.1 unit.1
  2.8 3.1 %collective-permute-start.3 = (bf16[800,128]{1,0:T(8,128)(2,1)S(1)}, bf16[800,128]{1,0:T(8,128)(2,1)S(1)}, u32[]{:S(2)}, u32[]{:S(2)}) collective-permute-start(bf16[800,128]{1,0:T(8,128)(2,1)S(1)} %unit.1), channel_id=1, source_target_pairs={{0,2},{1,3},{2,0},{3,1},{4,6},{5,7},{6,4},{7,5},{8,10},{9,11},{10,... | collective-permute-start | bytes 614408 | tf_op jit(solution)/shard_map/ppermute | solution.py:51
  5.9 0.8 %collective-permute-start.2 = (bf16[800,128]{1,0:T(8,128)(2,1)S(1)}, bf16[800,128]{1,0:T(8,128)(2,1)S(1)}, u32[]{:S(2)}, u32[]{:S(2)}) collective-permute-start(bf16[800,128]{1,0:T(8,128)(2,1)S(1)} %unit.1), channel_id=1, source_target_pairs={{0,3},{1,0},{2,1},{3,2},{4,7},{5,4},{6,5},{7,6},{8,11},{9,8},{10,9... | collective-permute-start | bytes 614408 | tf_op jit(solution)/shard_map/ppermute | solution.py:51
  6.7 0.7 %collective-permute-start.1 = (bf16[800,128]{1,0:T(8,128)(2,1)S(1)}, bf16[800,128]{1,0:T(8,128)(2,1)S(1)}, u32[]{:S(2)}, u32[]{:S(2)}) collective-permute-start(bf16[800,128]{1,0:T(8,128)(2,1)S(1)} %unit.1), channel_id=1, source_target_pairs={{0,1},{1,2},{2,3},{3,0},{4,5},{5,6},{6,7},{7,4},{8,9},{9,10},{10,1... | collective-permute-start | bytes 614408 | tf_op jit(solution)/shard_map/ppermute | solution.py:51
  7.3 0.1 pad_add_fusion.2.here_ref
  7.4 4.6 %points.1 = (f32[32,4,128,128]{3,2,1,0:T(8,128)S(1)}, f32[8,8,256]{2,1,0:T(8,128)S(1)}, bf16[768,1024]{1,0:T(8,128)(2,1)S(1)}) custom-call(s32[4]{0:T(128)S(1)} %pad_add_fusion.2.here_ref, f32[3,128,256]{2,1,0:T(8,128)} %bitcast.70, f32[128,256]{1,0:T(8,128)} %areas_ref.1, bf16[768,1024]{1,0:T(8,128)(2,1)} %couplings_ref.1), custom_call_target="tpu_custom_call" | custom-call | tf_op jit(solution)/shard_map/points/pallas_call | solution.py:177
  12.0 0.0 collective-permute-done.3
  12.0 0.0 collective-permute-done.2
  12.1 0.7 %collective-permute-done.1 = bf16[800,128]{1,0:T(8,128)(2,1)S(1)} collective-permute-done((bf16[800,128]{1,0:T(8,128)(2,1)S(1)}, bf16[800,128]{1,0:T(8,128)(2,1)S(1)}, u32[]{:S(2)}, u32[]{:S(2)}) %collective-permute-start.1) | collective-permute-done | bytes 204832 | tf_op jit(solution)/shard_map/ppermute | solution.py:51
  12.8 0.0 copy-done.1
  12.8 0.1 compare_reduce_fusion.2
  12.9 0.2 fusion.27
  13.1 0.0 copy-done.2
  13.1 0.1 bitcast_select_fusion.1
  13.3 2.3 %collective-permute-start.5 = (bf16[1600,128]{1,0:T(8,128)(2,1)S(1)}, bf16[1600,128]{1,0:T(8,128)(2,1)S(1)}, u32[]{:S(2)}, u32[]{:S(2)}) collective-permute-start(bf16[1600,128]{1,0:T(8,128)(2,1)S(1)} %constant_dynamic-update-slice_fusion.2.refs_1_), channel_id=1, source_target_pairs={{0,12},{1,13},{2,14},{3,15},{4,0},{5,1},{6,2},{7,3},{8,4},{9,5},{1... | collective-permute-start | bytes 1228808 | tf_op jit(solution)/shard_map/ppermute | solution.py:56
  15.6 0.1 collective-permute-start.4
  15.6 0.9 %coupling_blocks.1 = bf16[64,2048]{1,0:T(8,128)(2,1)S(1)} custom-call(s32[1,768]{1,0:T(1,128)S(1)} %get-tuple-element.90.forward_ref, s32[1,768]{1,0:T(1,128)S(1)} %get-tuple-element.89.backward_ref, bf16[768,1024]{1,0:T(8,128)(2,1)S(1)} %get-tuple-element.56.couplings_ref, bf16[1024,1024]{1,0:T(8,128)(2,1)S(1)} %get-tuple-element.57.flip_ref), custom_call_target="tpu_custom_call" | custom-call | tf_op jit(solution)/shard_map/coupling_blocks/pallas_call | solution.py:215
  16.6 0.3 collective-permute-start.6
  16.8 2.6 %collective-permute-start.7 = (bf16[1600,128]{1,0:T(8,128)(2,1)S(1)}, bf16[1600,128]{1,0:T(8,128)(2,1)S(1)}, u32[]{:S(2)}, u32[]{:S(2)}) collective-permute-start(bf16[1600,128]{1,0:T(8,128)(2,1)S(1)} %constant_dynamic-update-slice_fusion.refs_0_), channel_id=1, source_target_pairs={{0,12},{1,13},{2,14},{3,15},{4,0},{5,1},{6,2},{7,3},{8,4},{9,5},{1... | collective-permute-start | bytes 1228808 | tf_op jit(solution)/shard_map/ppermute | solution.py:56
  19.4 0.2 fusion.2.counts
  19.6 5.7 %near_first.1 = (f32[8,768,128]{2,1,0:T(8,128)S(1)}, f32[4,64,128]{2,1,0:T(8,128)S(1)}) custom-call(s32[8,32]{1,0:T(8,128)S(1)} %fusion.2.counts, f32[8,8,256]{2,1,0:T(8,128)S(1)} %get-tuple-element.49.targets, f32[32,4,128,128]{3,2,1,0:T(8,128)S(1)} %get-tuple-element.50.spread, bf16[1600,128]{1,0:T(8,128)(2,1)S(1)} %constant_dynamic-update-slice_fusion.refs_0_, ...), custom_call_target="tpu_custom_call" | custom-call | flops 2000000000 | bytes 8000000 | tf_op jit(solution)/shard_map/near_first/pallas_call | solution.py:384
  25.3 0.0 collective-permute-done.5.refs_3_
  25.3 0.0 collective-permute-done.4.refs_0_
  25.3 0.1 collective-permute-start.8
  25.4 2.7 %collective-permute-start.9 = (bf16[1600,128]{1,0:T(8,128)(2,1)S(1)}, bf16[1600,128]{1,0:T(8,128)(2,1)S(1)}, u32[]{:S(2)}, u32[]{:S(2)}) collective-permute-start(bf16[1600,128]{1,0:T(8,128)(2,1)S(1)} %collective-permute-done.5.refs_3_), channel_id=1, source_target_pairs={{0,12},{1,13},{2,14},{3,15},{4,0},{5,1},{6,2},{7,3},{8,4},{9,5},{1... | collective-permute-start | bytes 1228808 | tf_op jit(solution)/shard_map/ppermute | solution.py:56
  28.1 0.2 collective-permute-done.6.refs_1_
  28.3 0.0 collective-permute-done.7.refs_2_
  28.3 5.4 %near_middle.1 = (f32[6,768,128]{2,1,0:T(8,128)S(1)}, f32[4,64,128]{2,1,0:T(8,128)S(1)}) custom-call(s32[8,32]{1,0:T(8,128)S(1)} %fusion.2.counts, f32[8,8,256]{2,1,0:T(8,128)S(1)} %get-tuple-element.49.targets, f32[32,4,128,128]{3,2,1,0:T(8,128)S(1)} %get-tuple-element.50.spread, bf16[1600,128]{1,0:T(8,128)(2,1)S(1)} %collective-permute-done.4.refs_0_, ...), custom_call_target="tpu_custom_call" | custom-call | flops 4000000000 | bytes 8000000 | tf_op jit(solution)/shard_map/near_middle/pallas_call | solution.py:384
  33.7 0.0 collective-permute-done.8.refs_0_.refs_4_
  33.7 0.0 collective-permute-done.9.refs_1_.refs_5_
  33.7 3.2 %near_send.1 = (bf16[3,800,128]{2,1,0:T(8,128)(2,1)S(1)}, f32[4,64,128]{2,1,0:T(8,128)S(1)}) custom-call(s32[8,32]{1,0:T(8,128)S(1)} %fusion.2.counts, f32[8,8,256]{2,1,0:T(8,128)S(1)} %get-tuple-element.49.targets, f32[32,4,128,128]{3,2,1,0:T(8,128)S(1)} %get-tuple-element.50.spread, bf16[1600,128]{1,0:T(8,128)(2,1)S(1)} %collective-permute-done.8.refs_0_.refs_4_, ...), custom_call_target="tpu_custom_call" | custom-call | flops 2000000000 | bytes 8000000 | tf_op jit(solution)/shard_map/near_send/pallas_call | solution.py:384
  36.9 4.9 %collective-permute-start.10 = (bf16[3,800,128]{2,1,0:T(8,128)(2,1)S(1)}, bf16[3,800,128]{2,1,0:T(8,128)(2,1)S(1)}, u32[]{:S(2)}, u32[]{:S(2)}) collective-permute-start(bf16[3,800,128]{2,1,0:T(8,128)(2,1)S(1)} %get-tuple-element.70), channel_id=1, source_target_pairs={{0,16},{1,17},{2,18},{3,19},{4,20},{5,21},{6,22},{7,23},{8,24},{9,... | collective-permute-start | bytes 1843208 | tf_op jit(solution)/shard_map/ppermute | solution.py:46
  41.8 2.7 %near_keep.1 = f32[3,800,128]{2,1,0:T(8,128)S(1)} custom-call(s32[8,32]{1,0:T(8,128)S(1)} %fusion.2.counts, f32[8,8,256]{2,1,0:T(8,128)S(1)} %get-tuple-element.49.targets, f32[32,4,128,128]{3,2,1,0:T(8,128)S(1)} %get-tuple-element.50.spread, bf16[1600,128]{1,0:T(8,128)(2,1)S(1)} %collective-permute-done.8.refs_0_.refs_4_, ...), custom_call_target="tpu_custom_call" | custom-call | flops 2000000000 | bytes 8000000 | tf_op jit(solution)/shard_map/near_keep/pallas_call | solution.py:384
  44.6 0.0 collective-permute-done.10
  44.6 0.1 fusion.9
  44.7 0.0 copy-start
  44.7 2.4 %collective-permute-start.11 = (bf16[800,128]{1,0:T(8,128)(2,1)S(1)}, bf16[800,128]{1,0:T(8,128)(2,1)S(1)}, u32[]{:S(2)}, u32[]{:S(2)}) collective-permute-start(bf16[800,128]{1,0:T(8,128)(2,1)S(1)} %get-tuple-element.74), channel_id=1, source_target_pairs={{0,32},{1,33},{2,34},{3,35},{4,36},{5,37},{6,38},{7,39},{8,40},{9,... | collective-permute-start | bytes 614408 | tf_op jit(solution)/shard_map/ppermute | solution.py:60
  47.1 2.6 %collective-permute-start.12 = (bf16[800,128]{1,0:T(8,128)(2,1)S(1)}, bf16[800,128]{1,0:T(8,128)(2,1)S(1)}, u32[]{:S(2)}, u32[]{:S(2)}) collective-permute-start(bf16[800,128]{1,0:T(8,128)(2,1)S(1)} %get-tuple-element.75), channel_id=1, source_target_pairs={{0,96},{1,97},{2,98},{3,99},{4,100},{5,101},{6,102},{7,103},{8,104... | collective-permute-start | bytes 614408 | tf_op jit(solution)/shard_map/ppermute | solution.py:60
  49.7 1.1 %collective-permute-start.13 = (bf16[800,128]{1,0:T(8,128)(2,1)S(1)}, bf16[800,128]{1,0:T(8,128)(2,1)S(1)}, u32[]{:S(2)}, u32[]{:S(2)}) collective-permute-start(bf16[800,128]{1,0:T(8,128)(2,1)S(1)} %get-tuple-element.76), channel_id=1, source_target_pairs={{0,64},{1,65},{2,66},{3,67},{4,68},{5,69},{6,70},{7,71},{8,72},{9,... | collective-permute-start | bytes 614408 | tf_op jit(solution)/shard_map/ppermute | solution.py:60
  50.8 3.3 %near_own.1 = (f32[2,800,128]{2,1,0:T(8,128)S(1)}, bf16[2,800,128]{2,1,0:T(8,128)(2,1)S(1)}) custom-call(s32[8,32]{1,0:T(8,128)S(1)} %fusion.2.counts, f32[8,8,256]{2,1,0:T(8,128)S(1)} %get-tuple-element.49.targets, f32[32,4,128,128]{3,2,1,0:T(8,128)S(1)} %get-tuple-element.50.spread, bf16[1600,128]{1,0:T(8,128)(2,1)S(1)} %collective-permute-done.4.refs_0_, ...), custom_call_target="tpu_custom_call" | custom-call | flops 6000000000 | bytes 8000000 | tf_op jit(solution)/shard_map/near_own/pallas_call | solution.py:384
  54.1 3.7 %all_to_all.5.swapped = bf16[2,800,128]{2,1,0:T(8,128)(2,1)S(1)} all-to-all(bf16[2,800,128]{2,1,0:T(8,128)(2,1)S(1)} %get-tuple-element.73), channel_id=1, replica_groups={{0,16},{32,48},{64,80},{96,112},{1,17},{33,49},{65,81},{97,113},{2,18},..., dimensions={0} | all-to-all | bytes 819200 | tf_op jit(solution)/shard_map/all_to_all | solution.py:530
  57.7 0.0 collective-permute-done.11.one
  57.7 0.9 %collective-permute-done.12.two = bf16[800,128]{1,0:T(8,128)(2,1)S(1)} collective-permute-done((bf16[800,128]{1,0:T(8,128)(2,1)S(1)}, bf16[800,128]{1,0:T(8,128)(2,1)S(1)}, u32[]{:S(2)}, u32[]{:S(2)}) %collective-permute-start.12) | collective-permute-done | bytes 204832 | tf_op jit(solution)/shard_map/ppermute | solution.py:60
  58.6 1.5 %collective-permute-done.13.three = bf16[800,128]{1,0:T(8,128)(2,1)S(1)} collective-permute-done((bf16[800,128]{1,0:T(8,128)(2,1)S(1)}, bf16[800,128]{1,0:T(8,128)(2,1)S(1)}, u32[]{:S(2)}, u32[]{:S(2)}) %collective-permute-start.13) | collective-permute-done | bytes 204832 | tf_op jit(solution)/shard_map/ppermute | solution.py:60
  60.2 1.0 %sum_and_expand.1 = bf16[1,3,256,128]{3,2,1,0:T(8,128)(2,1)} custom-call(s32[1]{0:T(128)} %bitcast.core_ref.core, f32[2,800,128]{2,1,0:T(8,128)S(1)} %get-tuple-element.72.keep, bf16[2,800,128]{2,1,0:T(8,128)(2,1)S(1)} %all_to_all.5.swapped, bf16[800,128]{1,0:T(8,128)(2,1)S(1)} %collective-permute-done.11.one, ...), custom_call_target="tpu_custom_call" | custom-call | tf_op jit(solution)/shard_map/sum_and_expand/pallas_call | solution.py:427
  (13 shorter events, 0.1 us)
Async XLA Ops:
  0.0 13.1 %copy-start.2 = (s32[768,2]{0,1:T(2,128)S(1)}, s32[768,2]{0,1:T(2,128)}, u32[]{:S(2)}) copy-start(s32[768,2]{0,1:T(2,128)} %param.12) | copy-start | bytes 18436
  0.0 12.8 %copy-start.1 = (s32[1920,2]{0,1:T(2,128)S(1)}, s32[1920,2]{0,1:T(2,128)}, u32[]{:S(2)}) copy-start(s32[1920,2]{0,1:T(2,128)} %param.11) | copy-start | bytes 46084
  0.0 2.7 %collective-permute-start = (bf16[1,3,256,128]{3,2,1,0:T(8,128)(2,1)}, bf16[1,3,256,128]{3,2,1,0:T(8,128)(2,1)S(1)}, u32[]{:S(2)}, u32[]{:S(2)}) collective-permute-start(bf16[1,3,256,128]{3,2,1,0:T(8,128)(2,1)} %dens_ref.1), channel_id=1, source_target_pairs={{0,16},{1,17},{2,18},{3,19},{4,20},{5,21},{6,22},{7,23},{8,24},{9,... | collective-permute-start | bytes 589832 | tf_op jit(solution)/shard_map/ppermute | solution.py:46
  2.8 9.2 %collective-permute-start.3 = (bf16[800,128]{1,0:T(8,128)(2,1)S(1)}, bf16[800,128]{1,0:T(8,128)(2,1)S(1)}, u32[]{:S(2)}, u32[]{:S(2)}) collective-permute-start(bf16[800,128]{1,0:T(8,128)(2,1)S(1)} %unit.1), channel_id=1, source_target_pairs={{0,2},{1,3},{2,0},{3,1},{4,6},{5,7},{6,4},{7,5},{8,10},{9,11},{10,... | collective-permute-start | bytes 614408 | tf_op jit(solution)/shard_map/ppermute | solution.py:51
  5.9 6.2 %collective-permute-start.2 = (bf16[800,128]{1,0:T(8,128)(2,1)S(1)}, bf16[800,128]{1,0:T(8,128)(2,1)S(1)}, u32[]{:S(2)}, u32[]{:S(2)}) collective-permute-start(bf16[800,128]{1,0:T(8,128)(2,1)S(1)} %unit.1), channel_id=1, source_target_pairs={{0,3},{1,0},{2,1},{3,2},{4,7},{5,4},{6,5},{7,6},{8,11},{9,8},{10,9... | collective-permute-start | bytes 614408 | tf_op jit(solution)/shard_map/ppermute | solution.py:51
  6.7 6.1 %collective-permute-start.1 = (bf16[800,128]{1,0:T(8,128)(2,1)S(1)}, bf16[800,128]{1,0:T(8,128)(2,1)S(1)}, u32[]{:S(2)}, u32[]{:S(2)}) collective-permute-start(bf16[800,128]{1,0:T(8,128)(2,1)S(1)} %unit.1), channel_id=1, source_target_pairs={{0,1},{1,2},{2,3},{3,0},{4,5},{5,6},{6,7},{7,4},{8,9},{9,10},{10,1... | collective-permute-start | bytes 614408 | tf_op jit(solution)/shard_map/ppermute | solution.py:51
  13.3 12.0 %collective-permute-start.5 = (bf16[1600,128]{1,0:T(8,128)(2,1)S(1)}, bf16[1600,128]{1,0:T(8,128)(2,1)S(1)}, u32[]{:S(2)}, u32[]{:S(2)}) collective-permute-start(bf16[1600,128]{1,0:T(8,128)(2,1)S(1)} %constant_dynamic-update-slice_fusion.2.refs_1_), channel_id=1, source_target_pairs={{0,12},{1,13},{2,14},{3,15},{4,0},{5,1},{6,2},{7,3},{8,4},{9,5},{1... | collective-permute-start | bytes 1228808 | tf_op jit(solution)/shard_map/ppermute | solution.py:56
  15.6 9.8 %collective-permute-start.4 = (bf16[1600,128]{1,0:T(8,128)(2,1)S(1)}, bf16[1600,128]{1,0:T(8,128)(2,1)S(1)}, u32[]{:S(2)}, u32[]{:S(2)}) collective-permute-start(bf16[1600,128]{1,0:T(8,128)(2,1)S(1)} %constant_dynamic-update-slice_fusion.refs_0_), channel_id=1, source_target_pairs={{0,4},{1,5},{2,6},{3,7},{4,8},{5,9},{6,10},{7,11},{8,12},{9,13},{1... | collective-permute-start | bytes 1228808 | tf_op jit(solution)/shard_map/ppermute | solution.py:56
  16.6 11.8 %collective-permute-start.6 = (bf16[1600,128]{1,0:T(8,128)(2,1)S(1)}, bf16[1600,128]{1,0:T(8,128)(2,1)S(1)}, u32[]{:S(2)}, u32[]{:S(2)}) collective-permute-start(bf16[1600,128]{1,0:T(8,128)(2,1)S(1)} %constant_dynamic-update-slice_fusion.2.refs_1_), channel_id=1, source_target_pairs={{0,4},{1,5},{2,6},{3,7},{4,8},{5,9},{6,10},{7,11},{8,12},{9,13},{1... | collective-permute-start | bytes 1228808 | tf_op jit(solution)/shard_map/ppermute | solution.py:56
  16.8 11.5 %collective-permute-start.7 = (bf16[1600,128]{1,0:T(8,128)(2,1)S(1)}, bf16[1600,128]{1,0:T(8,128)(2,1)S(1)}, u32[]{:S(2)}, u32[]{:S(2)}) collective-permute-start(bf16[1600,128]{1,0:T(8,128)(2,1)S(1)} %constant_dynamic-update-slice_fusion.refs_0_), channel_id=1, source_target_pairs={{0,12},{1,13},{2,14},{3,15},{4,0},{5,1},{6,2},{7,3},{8,4},{9,5},{1... | collective-permute-start | bytes 1228808 | tf_op jit(solution)/shard_map/ppermute | solution.py:56
  25.3 8.4 %collective-permute-start.8 = (bf16[1600,128]{1,0:T(8,128)(2,1)S(1)}, bf16[1600,128]{1,0:T(8,128)(2,1)S(1)}, u32[]{:S(2)}, u32[]{:S(2)}) collective-permute-start(bf16[1600,128]{1,0:T(8,128)(2,1)S(1)} %collective-permute-done.4.refs_0_), channel_id=1, source_target_pairs={{0,4},{1,5},{2,6},{3,7},{4,8},{5,9},{6,10},{7,11},{8,12},{9,13},{1... | collective-permute-start | bytes 1228808 | tf_op jit(solution)/shard_map/ppermute | solution.py:56
  25.4 8.3 %collective-permute-start.9 = (bf16[1600,128]{1,0:T(8,128)(2,1)S(1)}, bf16[1600,128]{1,0:T(8,128)(2,1)S(1)}, u32[]{:S(2)}, u32[]{:S(2)}) collective-permute-start(bf16[1600,128]{1,0:T(8,128)(2,1)S(1)} %collective-permute-done.5.refs_3_), channel_id=1, source_target_pairs={{0,12},{1,13},{2,14},{3,15},{4,0},{5,1},{6,2},{7,3},{8,4},{9,5},{1... | collective-permute-start | bytes 1228808 | tf_op jit(solution)/shard_map/ppermute | solution.py:56
  36.9 7.6 %collective-permute-start.10 = (bf16[3,800,128]{2,1,0:T(8,128)(2,1)S(1)}, bf16[3,800,128]{2,1,0:T(8,128)(2,1)S(1)}, u32[]{:S(2)}, u32[]{:S(2)}) collective-permute-start(bf16[3,800,128]{2,1,0:T(8,128)(2,1)S(1)} %get-tuple-element.70), channel_id=1, source_target_pairs={{0,16},{1,17},{2,18},{3,19},{4,20},{5,21},{6,22},{7,23},{8,24},{9,... | collective-permute-start | bytes 1843208 | tf_op jit(solution)/shard_map/ppermute | solution.py:46
  44.7 15.5 %copy-start = (bf16[1,32,3,256]{3,1,2,0:T(8,128)(2,1)S(1)}, bf16[1,32,3,256]{3,1,2,0:T(8,128)(2,1)}, u32[]{:S(2)}) copy-start(bf16[1,32,3,256]{3,1,2,0:T(8,128)(2,1)} %param.10) | copy-start | bytes 147460
  44.7 13.0 %collective-permute-start.11 = (bf16[800,128]{1,0:T(8,128)(2,1)S(1)}, bf16[800,128]{1,0:T(8,128)(2,1)S(1)}, u32[]{:S(2)}, u32[]{:S(2)}) collective-permute-start(bf16[800,128]{1,0:T(8,128)(2,1)S(1)} %get-tuple-element.74), channel_id=1, source_target_pairs={{0,32},{1,33},{2,34},{3,35},{4,36},{5,37},{6,38},{7,39},{8,40},{9,... | collective-permute-start | bytes 614408 | tf_op jit(solution)/shard_map/ppermute | solution.py:60
  47.1 11.5 %collective-permute-start.12 = (bf16[800,128]{1,0:T(8,128)(2,1)S(1)}, bf16[800,128]{1,0:T(8,128)(2,1)S(1)}, u32[]{:S(2)}, u32[]{:S(2)}) collective-permute-start(bf16[800,128]{1,0:T(8,128)(2,1)S(1)} %get-tuple-element.75), channel_id=1, source_target_pairs={{0,96},{1,97},{2,98},{3,99},{4,100},{5,101},{6,102},{7,103},{8,104... | collective-permute-start | bytes 614408 | tf_op jit(solution)/shard_map/ppermute | solution.py:60
  49.7 10.5 %collective-permute-start.13 = (bf16[800,128]{1,0:T(8,128)(2,1)S(1)}, bf16[800,128]{1,0:T(8,128)(2,1)S(1)}, u32[]{:S(2)}, u32[]{:S(2)}) collective-permute-start(bf16[800,128]{1,0:T(8,128)(2,1)S(1)} %get-tuple-element.76), channel_id=1, source_target_pairs={{0,64},{1,65},{2,66},{3,67},{4,68},{5,69},{6,70},{7,71},{8,72},{9,... | collective-permute-start | bytes 614408 | tf_op jit(solution)/shard_map/ppermute | solution.py:60
